TPU v7x, 32 devices: a whole 2x2x4 slice. The times are simulated.
32 devices in a mesh: groups: 2 (over y), enc: 16 (over z, x, core), dp: 1.
Axes of the slice: x: 2, y: 2, z: 4, core: 2. Of those that a mesh axis runs over, the one named last changes fastest.
Arguments:
- tokens: bfloat16 [2, 2048, 1280], P(('groups', 'dp'), 'enc'), parts along dimension 0
- cotangent: bfloat16 [2, 2048, 1280], P(('groups', 'dp'), 'enc'), parts along dimension 0
- page_of_band: int32 [2, 16], P(('groups', 'dp'), 'enc'), parts along dimension 0, may hold values from 0 to 3, never falling along the last dimension, each value on 1 to 5 neighbouring positions
- window_order: int32 [2, 16, 128], P(('groups', 'dp'), 'enc'), parts along dimension 0, may hold values from 0 to 127, each once within a row
- qkv_weight: bfloat16 [2, 1280, 1920], P(None, ('enc', 'dp'))
- out_weight: bfloat16 [2, 640, 1280], P(None, None, ('enc', 'dp')), may hold values from -0.25 to 0.25
- norm_gain: float32 [2, 1280], replicated, may hold values from 0.1 to 1.9
Outputs:
- mixed: bfloat16 [2, 2048, 1280], P(('groups', 'dp'), 'enc'), parts along dimension 0
- grad_tokens: float32 [2, 2048, 1280], P(('groups', 'dp'), 'enc'), parts along dimension 0
- grad_gain: float32 [4, 1280], P('groups'), parts along dimension 0
There are 2 independent parts, one for each index of `groups`. A program takes and returns all parts, laid end to end along the dimension named above; an argument that names none is the same for every part. Nothing has to cross between parts.
Inputs may be any that keep to these rules, and one draw needn't show every extreme that they name: `page_of_band`: along a batch row page numbers never fall; each page covers 1 to 5 consecutive bands, some page exactly 5, and every number up to 3 is used. `window_order`: each band's row lists every position of the band once.
All inputs are finite; a program needn't handle non-finite values.
Results may differ from a plain program's by a relative error of at most 0.029.
Values may be sent and summed in bfloat16 or wider, within the bound.
A program may use at most 128 MiB of HBM per device.

v0:
```python
import jax
import jax.numpy as jnp
from jax import lax
from jax.sharding import PartitionSpec as P

HDIM = 80
HEADS = 8
WIN = 64


EPSILON = 1e-06
MASKED = -1e30


def shifted(value, axis, steps):
    count = lax.axis_size(axis)
    first, last = (max(0, -steps), min(count, count - steps))
    return lax.ppermute(value, axis, [(source, source + steps) for source in range(first, last)])


def normalize(inputs, gain_row):
    widened = inputs.astype(jnp.float32)
    inverse = lax.rsqrt(jnp.mean(widened * widened, axis=-1, keepdims=True) + EPSILON)
    return ((widened * inverse * gain_row).astype(jnp.bfloat16), inverse)


def norm_back(inputs, gain_row, inverse, grad_normed):
    widened = inputs.astype(jnp.float32)
    scaled = grad_normed * gain_row
    inner = jnp.mean(scaled * widened, axis=-1, keepdims=True)
    grad_inputs = inverse * scaled - widened * inverse**3 * inner
    grad_row = jnp.sum(grad_normed * widened * inverse, axis=0)
    return (grad_inputs, grad_row)


def split_heads(matrix):
    return matrix.reshape(matrix.shape[0], HEADS, HDIM).transpose(1, 0, 2)


def join_heads(stacked):
    return stacked.transpose(1, 0, 2).reshape(stacked.shape[1], -1)


def head_scores(head_query, head_key, allowed):
    factor = head_query.shape[-1] ** (-0.5)
    scores = (
        jnp.einsum("qd,kd->qk", head_query, head_key, preferred_element_type=jnp.float32) * factor
    )
    return jnp.where(allowed, scores, MASKED)


def head_core(head_query, head_key, head_value, head_grad, head_logsum, head_delta, allowed):
    scores = head_scores(head_query, head_key, allowed)
    probs = jnp.exp(scores - head_logsum[:, None])
    grad_probs = jnp.einsum("qd,kd->qk", head_grad, head_value, preferred_element_type=jnp.float32)
    grad_scores = (probs * (grad_probs - head_delta[:, None])).astype(jnp.bfloat16)
    return (probs, grad_scores)


def head_deltas(output, grad_out):
    return jnp.sum(
        split_heads(grad_out).astype(jnp.float32) * split_heads(output).astype(jnp.float32), axis=-1
    )


def attend_forward(queries, keys_all, values_all, allowed):

    def per_head(inputs):
        scores = head_scores(inputs[0], inputs[1], allowed)
        largest = jnp.max(scores, axis=-1, keepdims=True)
        logsum = largest + jnp.log(jnp.sum(jnp.exp(scores - largest), axis=-1, keepdims=True))
        probs = jnp.exp(scores - logsum).astype(jnp.bfloat16)
        output = jnp.einsum("qk,kd->qd", probs, inputs[2], preferred_element_type=jnp.float32)
        return (output, logsum[:, 0])

    output, logsum = lax.map(
        per_head, (split_heads(queries), split_heads(keys_all), split_heads(values_all))
    )
    return (join_heads(output).astype(jnp.bfloat16), logsum)


def attend_backward(queries, keys_all, values_all, grad_out, logsum, deltas, allowed):

    def per_head(inputs):
        head_query, head_key, head_value, head_grad, head_logsum, head_delta = inputs
        factor = head_query.shape[-1] ** (-0.5)
        probs, grad_scores = head_core(
            head_query, head_key, head_value, head_grad, head_logsum, head_delta, allowed
        )
        grad_value = jnp.einsum(
            "qk,qd->kd", probs.astype(jnp.bfloat16), head_grad, preferred_element_type=jnp.float32
        )
        grad_query = (
            jnp.einsum("qk,kd->qd", grad_scores, head_key, preferred_element_type=jnp.float32)
            * factor
        )
        grad_key = (
            jnp.einsum("qk,qd->kd", grad_scores, head_query, preferred_element_type=jnp.float32)
            * factor
        )
        return (grad_query, grad_key, grad_value)

    grads = lax.map(
        per_head,
        (
            split_heads(queries),
            split_heads(keys_all),
            split_heads(values_all),
            split_heads(grad_out),
            logsum,
            deltas,
        ),
    )
    return (join_heads(grads[0]), join_heads(grads[1]), join_heads(grads[2]))


def window_forward(queries, keys_all, values_all, band_order):
    band_rows = queries.shape[0]
    allowed = jnp.ones((WIN, WIN), dtype=jnp.bool_)

    def one_window(window_query, window_key, window_value):
        return attend_forward(window_query, window_key, window_value, allowed)

    grouped = [
        matrix[band_order].reshape(band_rows // WIN, WIN, -1)
        for matrix in (queries, keys_all, values_all)
    ]
    output, logsum = jax.vmap(one_window)(grouped[0], grouped[1], grouped[2])
    restored = (
        jnp.zeros((band_rows, output.shape[-1]), jnp.bfloat16)
        .at[band_order]
        .set(output.reshape(band_rows, -1))
    )
    return (restored, logsum)


def window_backward(queries, keys_all, values_all, output, grad_out, logsum, band_order):
    band_rows = queries.shape[0]
    allowed = jnp.ones((WIN, WIN), dtype=jnp.bool_)

    def one_window(
        window_query, window_key, window_value, window_output, window_grad, window_logsum
    ):
        deltas = head_deltas(window_output, window_grad)
        return attend_backward(
            window_query, window_key, window_value, window_grad, window_logsum, deltas, allowed
        )

    grouped = [
        matrix[band_order].reshape(band_rows // WIN, WIN, -1)
        for matrix in (queries, keys_all, values_all, output, grad_out)
    ]
    grads = jax.vmap(one_window)(grouped[0], grouped[1], grouped[2], grouped[3], grouped[4], logsum)
    return tuple(
        (
            jnp.zeros((band_rows, grad.shape[-1]), jnp.float32)
            .at[band_order]
            .set(grad.reshape(band_rows, -1))
            for grad in grads
        )
    )


def collect_near(pack, reach):
    lower_parts = []
    upper_parts = []
    moving_lower = pack
    moving_upper = pack
    for offset in range(1, reach):
        moving_lower = shifted((pack[0], pack[1], pack[2]), "enc", offset)
        moving_upper = shifted((pack[0], pack[1], pack[2]), "enc", -offset)
        lower_parts.append(moving_lower)
        upper_parts.append(moving_upper)
    return lower_parts[::-1] + [pack] + upper_parts


def shards(tokens, cotangent, page_of_band, window_order, qkv_weight, out_weight, norm_gain):
    reach = min(5, lax.axis_size("enc") // 2)
    inputs_row = tokens[0]
    grad_mixed = cotangent[0]
    band_rows = inputs_row.shape[0]
    own_tag = (page_of_band[0] + 1).astype(jnp.bfloat16)
    band_order = window_order[0, 0]
    full_qkv, full_out = (
        lax.all_gather(qkv_weight[0], ("enc", "dp"), axis=0, tiled=True),
        lax.all_gather(out_weight[0], ("enc", "dp"), axis=1, tiled=True),
    )
    window_qkv, window_out = (
        lax.all_gather(qkv_weight[1], ("enc", "dp"), axis=0, tiled=True),
        lax.all_gather(out_weight[1], ("enc", "dp"), axis=1, tiled=True),
    )
    columns = full_out.shape[0]
    normed_full, inverse_full = normalize(inputs_row, norm_gain[0])
    packed_full = jnp.dot(normed_full, full_qkv, preferred_element_type=jnp.float32).astype(
        jnp.bfloat16
    )
    query_full = packed_full[:, :columns]
    key_full = packed_full[:, columns : 2 * columns]
    value_full = packed_full[:, 2 * columns :]
    near = collect_near((key_full, value_full, own_tag), reach)
    near_keys = jnp.concatenate([entry[0] for entry in near], axis=0)
    near_values = jnp.concatenate([entry[1] for entry in near], axis=0)
    near_tags = jnp.concatenate(
        [jnp.broadcast_to(entry[2], (band_rows,)) for entry in near], axis=0
    )
    allowed = near_tags[None, :] == own_tag[:, None]
    att_full, logsum_full = attend_forward(query_full, near_keys, near_values, allowed)
    hidden = (
        inputs_row.astype(jnp.float32)
        + jnp.dot(att_full, full_out, preferred_element_type=jnp.float32)
    ).astype(jnp.bfloat16)
    normed_window, inverse_window = normalize(hidden, norm_gain[1])
    packed_window = jnp.dot(normed_window, window_qkv, preferred_element_type=jnp.float32).astype(
        jnp.bfloat16
    )
    query_window = packed_window[:, :columns]
    key_window = packed_window[:, columns : 2 * columns]
    value_window = packed_window[:, 2 * columns :]
    att_window, logsum_window = window_forward(query_window, key_window, value_window, band_order)
    mixed = (
        hidden.astype(jnp.float32)
        + jnp.dot(att_window, window_out, preferred_element_type=jnp.float32)
    ).astype(jnp.bfloat16)
    dout_window = jnp.einsum(
        "rd,hd->rh", grad_mixed, window_out, preferred_element_type=jnp.float32
    ).astype(jnp.bfloat16)
    grads_window = window_backward(
        query_window, key_window, value_window, att_window, dout_window, logsum_window, band_order
    )
    dpacked_window = jnp.concatenate(grads_window, axis=-1).astype(jnp.bfloat16)
    dnormed_window = jnp.einsum(
        "rc,dc->rd", dpacked_window, window_qkv, preferred_element_type=jnp.float32
    )
    hidden_part, gain_window = norm_back(hidden, norm_gain[1], inverse_window, dnormed_window)
    dhidden = grad_mixed.astype(jnp.float32) + hidden_part
    dout_full = jnp.einsum(
        "rd,hd->rh", dhidden.astype(jnp.bfloat16), full_out, preferred_element_type=jnp.float32
    ).astype(jnp.bfloat16)
    deltas_full = head_deltas(att_full, dout_full)
    grad_query_full, near_grad_keys, near_grad_values = attend_backward(
        query_full, near_keys, near_values, dout_full, logsum_full, deltas_full, allowed
    )
    slots_keys = near_grad_keys.reshape(2 * reach - 1, band_rows, -1)
    slots_values = near_grad_values.reshape(2 * reach - 1, band_rows, -1)
    grad_key_full = slots_keys[reach - 1]
    grad_value_full = slots_values[reach - 1]
    for offset in range(1, reach):
        from_above = (
            shifted(slots_keys[reach - 1 - offset].astype(jnp.bfloat16), "enc", -offset).astype(
                jnp.float32
            ),
            shifted(slots_values[reach - 1 - offset].astype(jnp.bfloat16), "enc", -offset).astype(
                jnp.float32
            ),
        )
        from_below = (
            shifted(slots_keys[reach - 1 + offset].astype(jnp.bfloat16), "enc", offset).astype(
                jnp.float32
            ),
            shifted(slots_values[reach - 1 + offset].astype(jnp.bfloat16), "enc", offset).astype(
                jnp.float32
            ),
        )
        grad_key_full = grad_key_full + from_above[0] + from_below[0]
        grad_value_full = grad_value_full + from_above[1] + from_below[1]
    dpacked_full = jnp.concatenate(
        [grad_query_full, grad_key_full, grad_value_full], axis=-1
    ).astype(jnp.bfloat16)
    dnormed_full = jnp.einsum(
        "rc,dc->rd", dpacked_full, full_qkv, preferred_element_type=jnp.float32
    )
    tokens_part, gain_full = norm_back(inputs_row, norm_gain[0], inverse_full, dnormed_full)
    grad_tokens = dhidden + tokens_part
    grad_gain = lax.psum(jnp.stack([gain_full, gain_window]), ("enc", "dp"))
    return (mixed[None], grad_tokens[None], grad_gain)


def solution(mesh):
    return jax.shard_map(
        shards,
        mesh=mesh,
        in_specs=(
            P(("groups", "dp"), "enc", None),
            P(("groups", "dp"), "enc", None),
            P(("groups", "dp"), "enc"),
            P(("groups", "dp"), "enc", None),
            P(None, ("enc", "dp"), None),
            P(None, None, ("enc", "dp")),
            P(),
        ),
        out_specs=(
            P(("groups", "dp"), "enc", None),
            P(("groups", "dp"), "enc", None),
            P("groups", None),
        ),
        check_vma=False,
    )
```

profile of v0, /device:TPU:0, one launch (start us, length us, event | category | flops | bytes accessed | tf_op | source)
XLA Modules:
  0.0 541.1 jit_solution(5555783950070945864)
XLA Ops:
  7.3 2.0 fusion.173
  16.7 13.8 %collective-permute-start = (bf16[1]{0:T(256)(128)(2,1)}, bf16[1]{0:T(256)(128)(2,1)}, u32[]{:S(2)}, u32[]{:S(2)}) collective-permute-start(bf16[1]{0:T(256)(128)(2,1)} %bitcast.29), channel_id=1, source_target_pairs={{0,4},{1,5},{2,6},{3,7},{4,8},{5,9},{6,10},{7,11},{8,12},{9,13},{1... | collective-permute-start | bytes 14 | tf_op jit(solution)/shard_map/ppermute | solution.py:18
  32.2 4.0 collective-permute-start.1
  36.8 6.0 %collective-permute-start.2 = (bf16[1]{0:T(256)(128)(2,1)}, bf16[1]{0:T(256)(128)(2,1)}, u32[]{:S(2)}, u32[]{:S(2)}) collective-permute-start(bf16[1]{0:T(256)(128)(2,1)} %bitcast.29), channel_id=1, source_target_pairs={{0,2},{1,3},{2,4},{3,5},{4,6},{5,7},{6,8},{7,9},{8,10},{9,11},{10,... | collective-permute-start | bytes 14 | tf_op jit(solution)/shard_map/ppermute | solution.py:18
  43.4 2.2 collective-permute-start.3
  49.8 17.7 %all-gather.9.cloned.1.call-done = bf16[1,1280,1920]{2,1,0:T(8,128)(2,1)} async-done(((bf16[1,80,1920]{2,1,0:T(8,128)(2,1)}), bf16[1,1280,1920]{2,1,0:T(8,128)(2,1)}) %all-gather.9.cloned.1.call-update) | async-done | bytes 4915216 | tf_op jit(solution)/shard_map/all_gather | solution.py:185
  67.5 3.4 fusion.95
  71.6 3.4 collective-permute-start.16
  75.0 2.8 collective-permute-start.8
  77.8 31.0 %all-gather.15.cloned.1.call-done = bf16[1,640,1280]{1,2,0:T(8,128)(2,1)} async-done(((bf16[1,640,80]{1,2,0:T(8,128)(2,1)}), bf16[1,640,1280]{1,2,0:T(8,128)(2,1)}) %all-gather.15.cloned.1.call-update) | async-done | bytes 1638416 | tf_op jit(solution)/shard_map/all_gather | solution.py:190
  116.4 4.9 collective-permute-start.9
  122.0 4.5 collective-permute-start.10
  126.6 2.1 collective-permute-start.11
  129.3 3.4 collective-permute-done.10
  132.8 3.8 collective-permute-start.17
  137.3 3.8 collective-permute-start.18
  148.2 2.3 collective-permute-done.20
  154.6 7.1 %collective-permute-done.12 = bf16[128,640]{1,0:T(8,128)(2,1)S(1)} collective-permute-done((bf16[128,640]{1,0:T(8,128)(2,1)}, bf16[128,640]{1,0:T(8,128)(2,1)S(1)}, u32[]{:S(2)}, u32[]{:S(2)}) %collective-permute-start.12) | collective-permute-done | bytes 163872 | tf_op jit(solution)/shard_map/ppermute | solution.py:18
  165.2 2.5 copy.53
  170.9 3.7 copy.49
  174.5 2.8 copy.52
  177.4 32.0 %while.56 = (s32[]{:T(128)}, bf16[8,128,80]{1,2,0:T(8,128)(2,1)S(1)}, f32[8,128]{1,0:T(8,128)}, pred[1,1152]{1,0:T(4,128)(4,1)S(1)}, bf16[8,128,80]{2,1,0:T(8,12...) while((s32[]{:T(128)}, bf16[8,128,80]{1,2,0:T(8,128)(2,1)S(1)}, ...), condition=%wide.region_4.5_spmd.clone, body=%wide.region_1.4_spmd.sunk.clone | while | flops 48217984 | bytes 2444122 | solution.py:76
  209.4 2.2 multiply_reduce_fusion.2
  212.5 3.3 fusion.98
  224.7 2.0 copy_bitcast_fusion.1
  228.5 20.6 %while.57 = (s32[]{:T(128)}, bf16[8,2,64,80]{3,2,1,0:T(8,128)(2,1)}, f32[8,2,64]{2,1,0:T(2,128)S(1)}, bf16[8,2,64,80]{3,2,1,0:T(8,128)(2,1)}, bf16[8,2,64,80]{3,2,1,0:T(8,128)(2,1)}, /*index=5*/bf16[8,2,64,80]{3,2,1,0:T(8,128)(2,1)}) while((s32[]{:T(128)}, bf16[8,2,64,80]{3,2,1,0:T(8,128)(2,1)}, f32[8,2,64]{2,1,0:T(2,128)S(1)}, ...), condition=%wide.region_9.10_spmd.clone, body=%wide.region_6.9_spmd.sunk.clone | while | flops 2670466 | bytes 270417 | solution.py:76
  256.0 2.0 reshape.305
  259.3 52.5 %while.58 = (s32[]{:T(128)}, f32[8,2,64,80]{3,2,1,0:T(8,128)}, f32[8,2,64,80]{3,2,1,0:T(8,128)}, f32[8,2,64,80]{3,2,1,0:T(8,128)}, bf16[8,2,64,80]{3,2,1,0:T(8,1...) while((s32[]{:T(128)}, f32[8,2,64,80]{3,2,1,0:T(8,128)}, ...), condition=%wide.region_13.14_spmd.clone, body=%wide.region_12.13_spmd.sunk.clone | while | flops 6623234 | bytes 581745 | solution.py:103
  311.8 2.2 copy.62
  314.0 2.0 reshape.374
  318.1 2.2 copy.60
  320.3 2.0 reshape.358
  324.5 2.1 copy.61
  326.6 2.0 reshape.366
  330.2 4.3 multiply_reduce_fusion
  339.9 59.0 %while.59 = (s32[]{:T(128)}, bf16[8,128,80]{1,2,0:T(8,128)(2,1)}, f32[8,1152,80]{1,2,0:T(8,128)}, f32[8,1152,80]{1,2,0:T(8,128)}, pred[1,1152]{1,0:T(4,128)(4,1)...) while((s32[]{:T(128)}, bf16[8,128,80]{1,2,0:T(8,128)(2,1)}, ...), condition=%wide.region_20.21_spmd.clone, body=%wide.region_19.20_spmd.sunk.clone | while | flops 119099392 | bytes 4436346 | solution.py:103
  398.9 2.1 bitcast_convert_fusion
  401.3 16.7 %collective-permute-start.39 = (bf16[128,640]{0,1:T(8,128)(2,1)S(1)}, bf16[128,640]{0,1:T(8,128)(2,1)S(1)}, u32[]{:S(2)}, u32[]{:S(2)}) collective-permute-start(bf16[128,640]{0,1:T(8,128)(2,1)S(1)} %bitcast.422), channel_id=1, source_target_pairs={{0,4},{1,5},{2,6},{3,7},{4,8},{5,9},{6,10},{7,11},{8,12},{9,13},{1... | collective-permute-start | bytes 491528 | tf_op jit(solution)/shard_map/ppermute | solution.py:18
  421.9 5.9 %collective-permute-start.37 = (bf16[128,640]{0,1:T(8,128)(2,1)S(1)}, bf16[128,640]{0,1:T(8,128)(2,1)S(1)}, u32[]{:S(2)}, u32[]{:S(2)}) collective-permute-start(bf16[128,640]{0,1:T(8,128)(2,1)S(1)} %bitcast.419), channel_id=1, source_target_pairs={{0,3},{1,4},{2,5},{3,6},{4,7},{5,8},{6,9},{7,10},{8,11},{9,12},{10... | collective-permute-start | bytes 491528 | tf_op jit(solution)/shard_map/ppermute | solution.py:18
  429.1 2.6 collective-permute-start.35
  433.3 3.7 collective-permute-start.33
  437.0 7.4 %collective-permute-start.31 = (bf16[128,640]{0,1:T(8,128)(2,1)S(1)}, bf16[128,640]{0,1:T(8,128)(2,1)S(1)}, u32[]{:S(2)}, u32[]{:S(2)}) collective-permute-start(bf16[128,640]{0,1:T(8,128)(2,1)S(1)} %bitcast.418), channel_id=1, source_target_pairs={{0,4},{1,5},{2,6},{3,7},{4,8},{5,9},{6,10},{7,11},{8,12},{9,13},{1... | collective-permute-start | bytes 491528 | tf_op jit(solution)/shard_map/ppermute | solution.py:18
  448.4 5.4 collective-permute-start.29
  455.2 3.2 collective-permute-start.27
  459.7 3.2 collective-permute-start.25
  464.3 5.1 collective-permute-done.26
  469.7 4.1 fusion.123
  473.8 59.5 %psum.7 = f32[2,1280]{1,0:T(2,128)} all-reduce(f32[2,1280]{1,0:T(2,128)S(1)} %pad_maximum_fusion), channel_id=1, replica_groups=mesh['groups'=2,'enc'=16,'dp'=1] {'enc','dp'}, use_global_device_ids=true, to_apply=%region_24.25 | all-reduce | flops 2560 | bytes 20480 | tf_op jit(solution)/shard_map/psum | solution.py:274
  (389 shorter events, 252.8 us)
Async XLA Ops:
  7.2 60.3 %all-gather.9.cloned.1.call-start = ((), (), s32[]{:S(2)}) async-start(), calls=%async_computation | async-start | bytes 5222400 | tf_op jit(solution)/shard_map/all_gather | solution.py:185
  9.3 99.5 %all-gather.15.cloned.1.call-start = ((), (), s32[]{:S(2)}) async-start(), calls=%async_computation.3 | async-start | bytes 1740800 | tf_op jit(solution)/shard_map/all_gather | solution.py:190
  10.1 199.3 %all-gather.11.cloned.1.call-start = ((), (), s32[]{:S(2)}) async-start(), calls=%async_computation.1 | async-start | bytes 1740800 | tf_op jit(solution)/shard_map/all_gather | solution.py:186
  10.8 201.7 %all-gather.13.cloned.1.call-start = ((), (), s32[]{:S(2)}) async-start(), calls=%async_computation.2 | async-start | bytes 5222400 | tf_op jit(solution)/shard_map/all_gather | solution.py:189
  11.5 37.5 %collective-permute-start.7 = (bf16[1]{0:T(256)(128)(2,1)}, bf16[1]{0:T(256)(128)(2,1)}, u32[]{:S(2)}, u32[]{:S(2)}) collective-permute-start(bf16[1]{0:T(256)(128)(2,1)} %bitcast.29), channel_id=1, source_target_pairs={{4,0},{5,1},{6,2},{7,3},{8,4},{9,5},{10,6},{11,7},{12,8},{13,9},{1... | collective-permute-start | bytes 14 | tf_op jit(solution)/shard_map/ppermute | solution.py:18
  12.8 35.5 %collective-permute-start.6 = (bf16[1]{0:T(256)(128)(2,1)}, bf16[1]{0:T(256)(128)(2,1)}, u32[]{:S(2)}, u32[]{:S(2)}) collective-permute-start(bf16[1]{0:T(256)(128)(2,1)} %bitcast.29), channel_id=1, source_target_pairs={{3,0},{4,1},{5,2},{6,3},{7,4},{8,5},{9,6},{10,7},{11,8},{12,9},{13... | collective-permute-start | bytes 14 | tf_op jit(solution)/shard_map/ppermute | solution.py:18
  14.1 33.6 %collective-permute-start.5 = (bf16[1]{0:T(256)(128)(2,1)}, bf16[1]{0:T(256)(128)(2,1)}, u32[]{:S(2)}, u32[]{:S(2)}) collective-permute-start(bf16[1]{0:T(256)(128)(2,1)} %bitcast.29), channel_id=1, source_target_pairs={{2,0},{3,1},{4,2},{5,3},{6,4},{7,5},{8,6},{9,7},{10,8},{11,9},{12,... | collective-permute-start | bytes 14 | tf_op jit(solution)/shard_map/ppermute | solution.py:18
  15.4 31.6 %collective-permute-start.4 = (bf16[1]{0:T(256)(128)(2,1)}, bf16[1]{0:T(256)(128)(2,1)}, u32[]{:S(2)}, u32[]{:S(2)}) collective-permute-start(bf16[1]{0:T(256)(128)(2,1)} %bitcast.29), channel_id=1, source_target_pairs={{1,0},{2,1},{3,2},{4,3},{5,4},{6,5},{7,6},{8,7},{9,8},{10,9},{11,1... | collective-permute-start | bytes 14 | tf_op jit(solution)/shard_map/ppermute | solution.py:18
  16.7 15.4 %collective-permute-start = (bf16[1]{0:T(256)(128)(2,1)}, bf16[1]{0:T(256)(128)(2,1)}, u32[]{:S(2)}, u32[]{:S(2)}) collective-permute-start(bf16[1]{0:T(256)(128)(2,1)} %bitcast.29), channel_id=1, source_target_pairs={{0,4},{1,5},{2,6},{3,7},{4,8},{5,9},{6,10},{7,11},{8,12},{9,13},{1... | collective-permute-start | bytes 14 | tf_op jit(solution)/shard_map/ppermute | solution.py:18
  32.2 4.6 collective-permute-start.1
  36.8 6.7 %collective-permute-start.2 = (bf16[1]{0:T(256)(128)(2,1)}, bf16[1]{0:T(256)(128)(2,1)}, u32[]{:S(2)}, u32[]{:S(2)}) collective-permute-start(bf16[1]{0:T(256)(128)(2,1)} %bitcast.29), channel_id=1, source_target_pairs={{0,2},{1,3},{2,4},{3,5},{4,6},{5,7},{6,8},{7,9},{8,10},{9,11},{10,... | collective-permute-start | bytes 14 | tf_op jit(solution)/shard_map/ppermute | solution.py:18
  43.4 2.9 collective-permute-start.3
  71.6 50.4 %collective-permute-start.16 = (bf16[128,640]{1,0:T(8,128)(2,1)S(1)}, bf16[128,640]{1,0:T(8,128)(2,1)S(1)}, u32[]{:S(2)}, u32[]{:S(2)}) collective-permute-start(bf16[128,640]{1,0:T(8,128)(2,1)S(1)} %get-tuple-element.351), channel_id=1, source_target_pairs={{0,4},{1,5},{2,6},{3,7},{4,8},{5,9},{6,10},{7,11},{8,12},{9,13},{1... | collective-permute-start | bytes 491528 | tf_op jit(solution)/shard_map/ppermute | solution.py:18
  75.0 41.4 %collective-permute-start.8 = (bf16[128,640]{1,0:T(8,128)(2,1)}, bf16[128,640]{1,0:T(8,128)(2,1)S(1)}, u32[]{:S(2)}, u32[]{:S(2)}) collective-permute-start(bf16[128,640]{1,0:T(8,128)(2,1)} %get-tuple-element.352), channel_id=1, source_target_pairs={{0,4},{1,5},{2,6},{3,7},{4,8},{5,9},{6,10},{7,11},{8,12},{9,13},{1... | collective-permute-start | bytes 491528 | tf_op jit(solution)/shard_map/ppermute | solution.py:18
  112.5 42.0 %collective-permute-start.23 = (bf16[128,640]{1,0:T(8,128)(2,1)S(1)}, bf16[128,640]{1,0:T(8,128)(2,1)S(1)}, u32[]{:S(2)}, u32[]{:S(2)}) collective-permute-start(bf16[128,640]{1,0:T(8,128)(2,1)S(1)} %get-tuple-element.351), channel_id=1, source_target_pairs={{4,0},{5,1},{6,2},{7,3},{8,4},{9,5},{10,6},{11,7},{12,8},{13,9},{1... | collective-permute-start | bytes 491528 | tf_op jit(solution)/shard_map/ppermute | solution.py:18
  113.8 39.4 %collective-permute-start.22 = (bf16[128,640]{1,0:T(8,128)(2,1)S(1)}, bf16[128,640]{1,0:T(8,128)(2,1)S(1)}, u32[]{:S(2)}, u32[]{:S(2)}) collective-permute-start(bf16[128,640]{1,0:T(8,128)(2,1)S(1)} %get-tuple-element.351), channel_id=1, source_target_pairs={{3,0},{4,1},{5,2},{6,3},{7,4},{8,5},{9,6},{10,7},{11,8},{12,9},{13... | collective-permute-start | bytes 491528 | tf_op jit(solution)/shard_map/ppermute | solution.py:18
  115.1 36.8 %collective-permute-start.21 = (bf16[128,640]{1,0:T(8,128)(2,1)S(1)}, bf16[128,640]{1,0:T(8,128)(2,1)S(1)}, u32[]{:S(2)}, u32[]{:S(2)}) collective-permute-start(bf16[128,640]{1,0:T(8,128)(2,1)S(1)} %get-tuple-element.351), channel_id=1, source_target_pairs={{2,0},{3,1},{4,2},{5,3},{6,4},{7,5},{8,6},{9,7},{10,8},{11,9},{12,... | collective-permute-start | bytes 491528 | tf_op jit(solution)/shard_map/ppermute | solution.py:18
  116.4 10.2 %collective-permute-start.9 = (bf16[128,640]{1,0:T(8,128)(2,1)}, bf16[128,640]{1,0:T(8,128)(2,1)S(1)}, u32[]{:S(2)}, u32[]{:S(2)}) collective-permute-start(bf16[128,640]{1,0:T(8,128)(2,1)} %get-tuple-element.352), channel_id=1, source_target_pairs={{0,3},{1,4},{2,5},{3,6},{4,7},{5,8},{6,9},{7,10},{8,11},{9,12},{10... | collective-permute-start | bytes 491528 | tf_op jit(solution)/shard_map/ppermute | solution.py:18
  122.0 10.8 %collective-permute-start.10 = (bf16[128,640]{1,0:T(8,128)(2,1)}, bf16[128,640]{1,0:T(8,128)(2,1)S(1)}, u32[]{:S(2)}, u32[]{:S(2)}) collective-permute-start(bf16[128,640]{1,0:T(8,128)(2,1)} %get-tuple-element.352), channel_id=1, source_target_pairs={{0,2},{1,3},{2,4},{3,5},{4,6},{5,7},{6,8},{7,9},{8,10},{9,11},{10,... | collective-permute-start | bytes 491528 | tf_op jit(solution)/shard_map/ppermute | solution.py:18
  126.6 10.7 %collective-permute-start.11 = (bf16[128,640]{1,0:T(8,128)(2,1)}, bf16[128,640]{1,0:T(8,128)(2,1)S(1)}, u32[]{:S(2)}, u32[]{:S(2)}) collective-permute-start(bf16[128,640]{1,0:T(8,128)(2,1)} %get-tuple-element.352), channel_id=1, source_target_pairs={{0,1},{1,2},{2,3},{3,4},{4,5},{5,6},{6,7},{7,8},{8,9},{9,10},{10,1... | collective-permute-start | bytes 491528 | tf_op jit(solution)/shard_map/ppermute | solution.py:18
  132.8 9.1 %collective-permute-start.17 = (bf16[128,640]{1,0:T(8,128)(2,1)S(1)}, bf16[128,640]{1,0:T(8,128)(2,1)S(1)}, u32[]{:S(2)}, u32[]{:S(2)}) collective-permute-start(bf16[128,640]{1,0:T(8,128)(2,1)S(1)} %get-tuple-element.351), channel_id=1, source_target_pairs={{0,3},{1,4},{2,5},{3,6},{4,7},{5,8},{6,9},{7,10},{8,11},{9,12},{10... | collective-permute-start | bytes 491528 | tf_op jit(solution)/shard_map/ppermute | solution.py:18
  137.3 7.6 %collective-permute-start.18 = (bf16[128,640]{1,0:T(8,128)(2,1)S(1)}, bf16[128,640]{1,0:T(8,128)(2,1)S(1)}, u32[]{:S(2)}, u32[]{:S(2)}) collective-permute-start(bf16[128,640]{1,0:T(8,128)(2,1)S(1)} %get-tuple-element.351), channel_id=1, source_target_pairs={{0,2},{1,3},{2,4},{3,5},{4,6},{5,7},{6,8},{7,9},{8,10},{9,11},{10,... | collective-permute-start | bytes 491528 | tf_op jit(solution)/shard_map/ppermute | solution.py:18
  141.8 4.4 collective-permute-start.19
  144.9 5.7 %collective-permute-start.20 = (bf16[128,640]{1,0:T(8,128)(2,1)S(1)}, bf16[128,640]{1,0:T(8,128)(2,1)S(1)}, u32[]{:S(2)}, u32[]{:S(2)}) collective-permute-start(bf16[128,640]{1,0:T(8,128)(2,1)S(1)} %get-tuple-element.351), channel_id=1, source_target_pairs={{1,0},{2,1},{3,2},{4,3},{5,4},{6,5},{7,6},{8,7},{9,8},{10,9},{11,1... | collective-permute-start | bytes 491528 | tf_op jit(solution)/shard_map/ppermute | solution.py:18
  146.2 23.1 %collective-permute-start.15 = (bf16[128,640]{1,0:T(8,128)(2,1)}, bf16[128,640]{1,0:T(8,128)(2,1)}, u32[]{:S(2)}, u32[]{:S(2)}) collective-permute-start(bf16[128,640]{1,0:T(8,128)(2,1)} %get-tuple-element.352), channel_id=1, source_target_pairs={{4,0},{5,1},{6,2},{7,3},{8,4},{9,5},{10,6},{11,7},{12,8},{13,9},{1... | collective-permute-start | bytes 491528 | tf_op jit(solution)/shard_map/ppermute | solution.py:18
  150.5 17.1 %collective-permute-start.14 = (bf16[128,640]{1,0:T(8,128)(2,1)}, bf16[128,640]{1,0:T(8,128)(2,1)}, u32[]{:S(2)}, u32[]{:S(2)}) collective-permute-start(bf16[128,640]{1,0:T(8,128)(2,1)} %get-tuple-element.352), channel_id=1, source_target_pairs={{3,0},{4,1},{5,2},{6,3},{7,4},{8,5},{9,6},{10,7},{11,8},{12,9},{13... | collective-permute-start | bytes 491528 | tf_op jit(solution)/shard_map/ppermute | solution.py:18
  151.9 10.6 %collective-permute-start.13 = (bf16[128,640]{1,0:T(8,128)(2,1)}, bf16[128,640]{1,0:T(8,128)(2,1)S(1)}, u32[]{:S(2)}, u32[]{:S(2)}) collective-permute-start(bf16[128,640]{1,0:T(8,128)(2,1)} %get-tuple-element.352), channel_id=1, source_target_pairs={{2,0},{3,1},{4,2},{5,3},{6,4},{7,5},{8,6},{9,7},{10,8},{11,9},{12,... | collective-permute-start | bytes 491528 | tf_op jit(solution)/shard_map/ppermute | solution.py:18
  153.2 8.4 %collective-permute-start.12 = (bf16[128,640]{1,0:T(8,128)(2,1)}, bf16[128,640]{1,0:T(8,128)(2,1)S(1)}, u32[]{:S(2)}, u32[]{:S(2)}) collective-permute-start(bf16[128,640]{1,0:T(8,128)(2,1)} %get-tuple-element.352), channel_id=1, source_target_pairs={{1,0},{2,1},{3,2},{4,3},{5,4},{6,5},{7,6},{8,7},{9,8},{10,9},{11,1... | collective-permute-start | bytes 491528 | tf_op jit(solution)/shard_map/ppermute | solution.py:18
  211.6 122.9 %copy-start.14 = (f32[128]{0:T(128)}, f32[128]{0:T(128)S(1)}, u32[]{:S(2)}) copy-start(f32[128]{0:T(128)S(1)} %get-tuple-element.358) | copy-start | bytes 1540
  211.6 122.9 %copy-start.18 = (f32[128]{0:T(128)}, f32[128]{0:T(128)S(1)}, u32[]{:S(2)}) copy-start(f32[128]{0:T(128)S(1)} %get-tuple-element.357) | copy-start | bytes 1540
  401.3 27.9 %collective-permute-start.39 = (bf16[128,640]{0,1:T(8,128)(2,1)S(1)}, bf16[128,640]{0,1:T(8,128)(2,1)S(1)}, u32[]{:S(2)}, u32[]{:S(2)}) collective-permute-start(bf16[128,640]{0,1:T(8,128)(2,1)S(1)} %bitcast.422), channel_id=1, source_target_pairs={{0,4},{1,5},{2,6},{3,7},{4,8},{5,9},{6,10},{7,11},{8,12},{9,13},{1... | collective-permute-start | bytes 491528 | tf_op jit(solution)/shard_map/ppermute | solution.py:18
  419.2 12.8 %collective-permute-start.32 = (bf16[128,640]{0,1:T(8,128)(2,1)S(1)}, bf16[128,640]{0,1:T(8,128)(2,1)S(1)}, u32[]{:S(2)}, u32[]{:S(2)}) collective-permute-start(bf16[128,640]{0,1:T(8,128)(2,1)S(1)} %bitcast.421), channel_id=1, source_target_pairs={{1,0},{2,1},{3,2},{4,3},{5,4},{6,5},{7,6},{8,7},{9,8},{10,9},{11,1... | collective-permute-start | bytes 491528 | tf_op jit(solution)/shard_map/ppermute | solution.py:18
  420.6 12.7 %collective-permute-start.38 = (bf16[128,640]{0,1:T(8,128)(2,1)S(1)}, bf16[128,640]{0,1:T(8,128)(2,1)S(1)}, u32[]{:S(2)}, u32[]{:S(2)}) collective-permute-start(bf16[128,640]{0,1:T(8,128)(2,1)S(1)} %bitcast.420), channel_id=1, source_target_pairs={{4,0},{5,1},{6,2},{7,3},{8,4},{9,5},{10,6},{11,7},{12,8},{13,9},{1... | collective-permute-start | bytes 491528 | tf_op jit(solution)/shard_map/ppermute | solution.py:18
  421.9 15.1 %collective-permute-start.37 = (bf16[128,640]{0,1:T(8,128)(2,1)S(1)}, bf16[128,640]{0,1:T(8,128)(2,1)S(1)}, u32[]{:S(2)}, u32[]{:S(2)}) collective-permute-start(bf16[128,640]{0,1:T(8,128)(2,1)S(1)} %bitcast.419), channel_id=1, source_target_pairs={{0,3},{1,4},{2,5},{3,6},{4,7},{5,8},{6,9},{7,10},{8,11},{9,12},{10... | collective-permute-start | bytes 491528 | tf_op jit(solution)/shard_map/ppermute | solution.py:18
  427.8 16.7 %collective-permute-start.36 = (bf16[128,640]{0,1:T(8,128)(2,1)S(1)}, bf16[128,640]{0,1:T(8,128)(2,1)S(1)}, u32[]{:S(2)}, u32[]{:S(2)}) collective-permute-start(bf16[128,640]{0,1:T(8,128)(2,1)S(1)} %bitcast.417), channel_id=1, source_target_pairs={{3,0},{4,1},{5,2},{6,3},{7,4},{8,5},{9,6},{10,7},{11,8},{12,9},{13... | collective-permute-start | bytes 491528 | tf_op jit(solution)/shard_map/ppermute | solution.py:18
  429.1 16.7 %collective-permute-start.35 = (bf16[128,640]{0,1:T(8,128)(2,1)S(1)}, bf16[128,640]{0,1:T(8,128)(2,1)S(1)}, u32[]{:S(2)}, u32[]{:S(2)}) collective-permute-start(bf16[128,640]{0,1:T(8,128)(2,1)S(1)} %bitcast.415), channel_id=1, source_target_pairs={{0,2},{1,3},{2,4},{3,5},{4,6},{5,7},{6,8},{7,9},{8,10},{9,11},{10,... | collective-permute-start | bytes 491528 | tf_op jit(solution)/shard_map/ppermute | solution.py:18
  432.0 16.4 %collective-permute-start.34 = (bf16[128,640]{0,1:T(8,128)(2,1)S(1)}, bf16[128,640]{0,1:T(8,128)(2,1)S(1)}, u32[]{:S(2)}, u32[]{:S(2)}) collective-permute-start(bf16[128,640]{0,1:T(8,128)(2,1)S(1)} %bitcast.413), channel_id=1, source_target_pairs={{2,0},{3,1},{4,2},{5,3},{6,4},{7,5},{8,6},{9,7},{10,8},{11,9},{12,... | collective-permute-start | bytes 491528 | tf_op jit(solution)/shard_map/ppermute | solution.py:18
  433.3 20.5 %collective-permute-start.33 = (bf16[128,640]{0,1:T(8,128)(2,1)S(1)}, bf16[128,640]{0,1:T(8,128)(2,1)S(1)}, u32[]{:S(2)}, u32[]{:S(2)}) collective-permute-start(bf16[128,640]{0,1:T(8,128)(2,1)S(1)} %bitcast.412), channel_id=1, source_target_pairs={{0,1},{1,2},{2,3},{3,4},{4,5},{5,6},{6,7},{7,8},{8,9},{9,10},{10,1... | collective-permute-start | bytes 491528 | tf_op jit(solution)/shard_map/ppermute | solution.py:18
  437.0 18.1 %collective-permute-start.31 = (bf16[128,640]{0,1:T(8,128)(2,1)S(1)}, bf16[128,640]{0,1:T(8,128)(2,1)S(1)}, u32[]{:S(2)}, u32[]{:S(2)}) collective-permute-start(bf16[128,640]{0,1:T(8,128)(2,1)S(1)} %bitcast.418), channel_id=1, source_target_pairs={{0,4},{1,5},{2,6},{3,7},{4,8},{5,9},{6,10},{7,11},{8,12},{9,13},{1... | collective-permute-start | bytes 491528 | tf_op jit(solution)/shard_map/ppermute | solution.py:18
  444.5 13.9 %collective-permute-start.24 = (bf16[128,640]{0,1:T(8,128)(2,1)S(1)}, bf16[128,640]{0,1:T(8,128)(2,1)S(1)}, u32[]{:S(2)}, u32[]{:S(2)}) collective-permute-start(bf16[128,640]{0,1:T(8,128)(2,1)S(1)} %bitcast.416), channel_id=1, source_target_pairs={{1,0},{2,1},{3,2},{4,3},{5,4},{6,5},{7,6},{8,7},{9,8},{10,9},{11,1... | collective-permute-start | bytes 491528 | tf_op jit(solution)/shard_map/ppermute | solution.py:18
  445.8 13.9 %collective-permute-start.30 = (bf16[128,640]{0,1:T(8,128)(2,1)S(1)}, bf16[128,640]{0,1:T(8,128)(2,1)S(1)}, u32[]{:S(2)}, u32[]{:S(2)}) collective-permute-start(bf16[128,640]{0,1:T(8,128)(2,1)S(1)} %bitcast.414), channel_id=1, source_target_pairs={{4,0},{5,1},{6,2},{7,3},{8,4},{9,5},{10,6},{11,7},{12,8},{13,9},{1... | collective-permute-start | bytes 491528 | tf_op jit(solution)/shard_map/ppermute | solution.py:18
  448.4 14.7 %collective-permute-start.29 = (bf16[128,640]{0,1:T(8,128)(2,1)S(1)}, bf16[128,640]{0,1:T(8,128)(2,1)S(1)}, u32[]{:S(2)}, u32[]{:S(2)}) collective-permute-start(bf16[128,640]{0,1:T(8,128)(2,1)S(1)} %bitcast.411), channel_id=1, source_target_pairs={{0,3},{1,4},{2,5},{3,6},{4,7},{5,8},{6,9},{7,10},{8,11},{9,12},{10... | collective-permute-start | bytes 491528 | tf_op jit(solution)/shard_map/ppermute | solution.py:18
  453.9 9.3 %collective-permute-start.28 = (bf16[128,640]{0,1:T(8,128)(2,1)S(1)}, bf16[128,640]{0,1:T(8,128)(2,1)S(1)}, u32[]{:S(2)}, u32[]{:S(2)}) collective-permute-start(bf16[128,640]{0,1:T(8,128)(2,1)S(1)} %bitcast.410), channel_id=1, source_target_pairs={{3,0},{4,1},{5,2},{6,3},{7,4},{8,5},{9,6},{10,7},{11,8},{12,9},{13... | collective-permute-start | bytes 491528 | tf_op jit(solution)/shard_map/ppermute | solution.py:18
  455.2 9.2 %collective-permute-start.27 = (bf16[128,640]{0,1:T(8,128)(2,1)S(1)}, bf16[128,640]{0,1:T(8,128)(2,1)S(1)}, u32[]{:S(2)}, u32[]{:S(2)}) collective-permute-start(bf16[128,640]{0,1:T(8,128)(2,1)S(1)} %bitcast.409), channel_id=1, source_target_pairs={{0,2},{1,3},{2,4},{3,5},{4,6},{5,7},{6,8},{7,9},{8,10},{9,11},{10,... | collective-permute-start | bytes 491528 | tf_op jit(solution)/shard_map/ppermute | solution.py:18
  458.4 11.0 %collective-permute-start.26 = (bf16[128,640]{0,1:T(8,128)(2,1)S(1)}, bf16[128,640]{0,1:T(8,128)(2,1)S(1)}, u32[]{:S(2)}, u32[]{:S(2)}) collective-permute-start(bf16[128,640]{0,1:T(8,128)(2,1)S(1)} %bitcast.408), channel_id=1, source_target_pairs={{2,0},{3,1},{4,2},{5,3},{6,4},{7,5},{8,6},{9,7},{10,8},{11,9},{12,... | collective-permute-start | bytes 491528 | tf_op jit(solution)/shard_map/ppermute | solution.py:18
  459.7 9.6 %collective-permute-start.25 = (bf16[128,640]{0,1:T(8,128)(2,1)S(1)}, bf16[128,640]{0,1:T(8,128)(2,1)S(1)}, u32[]{:S(2)}, u32[]{:S(2)}) collective-permute-start(bf16[128,640]{0,1:T(8,128)(2,1)S(1)} %bitcast.407), channel_id=1, source_target_pairs={{0,1},{1,2},{2,3},{3,4},{4,5},{5,6},{6,7},{7,8},{8,9},{9,10},{10,1... | collective-permute-start | bytes 491528 | tf_op jit(solution)/shard_map/ppermute | solution.py:18
  469.6 63.7 %copy-start.3 = (f32[128,1280]{1,0:T(8,128)S(1)}, f32[128,1280]{1,0:T(8,128)}, u32[]{:S(2)}) copy-start(f32[128,1280]{1,0:T(8,128)} %copy-done.2) | copy-start | bytes 1966084
  469.6 63.7 %copy-start.15 = (f32[128]{0:T(128)S(1)}, f32[128]{0:T(128)}, u32[]{:S(2)}) copy-start(f32[128]{0:T(128)} %copy-done.14) | copy-start | bytes 1540
  (21 other events, 445.5 us)
Sparse Core Ops, SparseCore 0:
  10.2 57.1 all-gather.8
  69.6 39.1 all-gather.14
  111.0 40.5 all-gather.10
  154.2 58.2 all-gather.12
where the time goes:
time: 550 us; the launch traced here: 541 us
  matrix products  166 us (30%)
  starting transfers between devices  127 us (23%)
  local copies, waits for them, and re-layouts  89.1 us (16%)
  waiting for transfers between devices  71 us (13%)
  blocking collectives  59.5 us (11%)
  between operations  15.5 us (3%)
  other arithmetic  12.1 us (2%)
    ppermute x40, starting transfers between devices, shifted(): lax.ppermute(value, axis, [(source, source + steps) for source in range(f...  127 us
    psum x1, blocking collectives, shards(): grad_gain = lax.psum(jnp.stack([gain_full, gain_window]), ('enc', 'dp'))  59.5 us
    dot_general x32, matrix products, head_scores(): jnp.einsum('qd,kd->qk', head_query, head_key, preferred_element_type=jnp....  32 us
    all_gather x1, waiting for transfers between devices, shards(): lax.all_gather(out_weight[1], ('enc', 'dp'), axis=1, tiled=True)  31 us
    dot_general x16, matrix products, per_head(): jnp.einsum('qk,qd->kd', grad_scores, head_query, preferred_element_type=j...  26.8 us
    dot_general x16, matrix products, per_head(): jnp.einsum('qk,qd->kd', probs.astype(jnp.bfloat16), head_grad, preferred_...  26.1 us
    dot_general x16, matrix products, per_head(): jnp.einsum('qk,kd->qd', probs, inputs[2], preferred_element_type=jnp.floa...  23 us
    ppermute x40, waiting for transfers between devices, shifted(): lax.ppermute(value, axis, [(source, source + steps) for source in range(f...  20.8 us
  transfers between devices with their start and end apart: 44, of which 10 were waited for; matrix products, arithmetic and copies ran while one was open for 13% of the time, Pallas kernels for 0%

commit v1 on v0

v1 whole, which is shorter than its diff:
```python
import functools

import jax
import jax.numpy as jnp
from jax import lax
from jax.experimental import pallas as pl
from jax.experimental.pallas import tpu as pltpu
from jax.sharding import PartitionSpec as P

HDIM = 80
HEADS = 8
WIN = 64
MAXB = 5
REACH = MAXB - 1
SLOTS = 2 * REACH + 1
EPSILON = 1e-06
MASKED = -1e30
FACTOR = HDIM**-0.5
OFFSETS = [d for k in range(REACH, 0, -1) for d in (k, -k)]
MESH = pl.DeviceIdType.MESH
VMEM = pl.BlockSpec(memory_space=pltpu.VMEM)
SMEM = pl.BlockSpec(memory_space=pltpu.SMEM)
LIMIT = 48 * 1024 * 1024
F32 = jnp.float32
BF16 = jnp.bfloat16


def mm(a, b):
    return jnp.dot(a, b, preferred_element_type=F32)


def mt(a, b):
    return lax.dot_general(a, b, (((1,), (1,)), ((), ())), preferred_element_type=F32)


def tm(a, b):
    return lax.dot_general(a, b, (((0,), (0,)), ((), ())), preferred_element_type=F32)


def normalize(x, gain_row):
    inverse = lax.rsqrt(jnp.mean(x * x, axis=-1, keepdims=True) + EPSILON)
    return (x * inverse * gain_row).astype(BF16), inverse


def norm_back(x, gain_row, inverse, grad_normed):
    scaled = grad_normed * gain_row
    inner = jnp.mean(scaled * x, axis=-1, keepdims=True)
    grad_inputs = inverse * scaled - x * (inverse * inverse * inverse) * inner
    grad_row = jnp.sum(grad_normed * (x * inverse), axis=0, keepdims=True)
    return grad_inputs, grad_row


def halo_kernel(count, *refs):
    n = lax.axis_size("enc")
    ins, outs = refs[:count], refs[count : 2 * count]
    send, recv = refs[2 * count :]
    me = lax.axis_index("enc")
    barrier = pltpu.get_barrier_semaphore()

    def valid(d):
        return me + d < n if d > 0 else me + d >= 0

    def copy(a, d, source, slot):
        return pltpu.make_async_remote_copy(
            src_ref=source,
            dst_ref=outs[a].at[slot],
            send_sem=send.at[a, REACH + d],
            recv_sem=recv.at[a, slot],
            device_id={"enc": me + d},
            device_id_type=MESH,
        )

    for d in OFFSETS:

        @pl.when(valid(d))
        def _():
            pl.semaphore_signal(barrier, inc=1, device_id={"enc": me + d}, device_id_type=MESH)

    pl.semaphore_wait(barrier, jnp.minimum(me, REACH) + jnp.minimum(n - 1 - me, REACH))

    for d in OFFSETS:

        @pl.when(valid(d))
        def _():
            for a in range(count):
                copy(a, d, ins[a], REACH - d).start()

    for a in range(count):
        outs[a][REACH] = ins[a][...]
    for d in OFFSETS:

        @pl.when(jnp.logical_not(valid(d)))
        def _():
            for a in range(count):
                outs[a][REACH + d] = jnp.zeros(ins[a].shape, ins[a].dtype)

    for d in OFFSETS:

        @pl.when(valid(d))
        def _():
            for a in range(count):
                copy(a, d, ins[a], REACH - d).wait_send()
                copy(a, d, ins[a], REACH + d).wait_recv()


def halo(collective_id, *arrays):
    count = len(arrays)
    return pl.pallas_call(
        functools.partial(halo_kernel, count),
        out_shape=[jax.ShapeDtypeStruct((SLOTS,) + a.shape, a.dtype) for a in arrays],
        in_specs=[VMEM] * count,
        out_specs=[VMEM] * count,
        scratch_shapes=[
            pltpu.SemaphoreType.DMA((count, SLOTS)),
            pltpu.SemaphoreType.DMA((count, SLOTS)),
        ],
        compiler_params=pltpu.CompilerParams(
            collective_id=collective_id, has_side_effects=True, vmem_limit_bytes=LIMIT
        ),
    )(*arrays)


def total_kernel(row_ref, out_ref, held, send, recv):
    n, m = lax.axis_size("enc"), lax.axis_size("dp")
    total = n * m
    me = lax.axis_index("enc") * m + lax.axis_index("dp")
    barrier = pltpu.get_barrier_semaphore()

    def peer(o):
        t = lax.rem(me + o, total)
        return {"enc": t // m, "dp": lax.rem(t, m)}

    def copy(o):
        return pltpu.make_async_remote_copy(
            src_ref=row_ref,
            dst_ref=held.at[o],
            send_sem=send.at[o],
            recv_sem=recv.at[o],
            device_id=peer(o),
            device_id_type=MESH,
        )

    def greet(o, c):
        pl.semaphore_signal(barrier, inc=1, device_id=peer(o), device_id_type=MESH)
        return c

    def begin(o, c):
        copy(o).start()
        return c

    def finish(o, c):
        copy(o).wait()
        return c

    lax.fori_loop(1, total, greet, 0)
    pl.semaphore_wait(barrier, total - 1)
    lax.fori_loop(1, total, begin, 0)
    held[0] = row_ref[...]
    lax.fori_loop(1, total, finish, 0)

    out_ref[...] = lax.fori_loop(1, total, lambda o, s: s + held[o], held[0])


def total_rows(rows):
    total = lax.axis_size("enc") * lax.axis_size("dp")
    return pl.pallas_call(
        total_kernel,
        out_shape=jax.ShapeDtypeStruct(rows.shape, rows.dtype),
        in_specs=[VMEM],
        out_specs=VMEM,
        scratch_shapes=[
            pltpu.VMEM((total,) + rows.shape, rows.dtype),
            pltpu.SemaphoreType.DMA((total,)),
            pltpu.SemaphoreType.DMA((total,)),
        ],
        compiler_params=pltpu.CompilerParams(
            collective_id=2, has_side_effects=True, vmem_limit_bytes=LIMIT
        ),
    )(rows)


def first_slot(tags):
    first = REACH
    for s in range(REACH - 1, -1, -1):
        first = jnp.where(tags[s] == tags[REACH], s, first)
    return first


def band_mask(tags, first, band):
    lanes = lax.broadcasted_iota(jnp.int32, (1, MAXB * band), 1)
    mask = lanes < 0
    for j in range(MAXB):
        same = (tags[first + j] == tags[REACH]).astype(jnp.int32)
        inside = jnp.logical_and(lanes >= j * band, lanes < (j + 1) * band)
        mask = jnp.logical_or(mask, jnp.logical_and(inside, same == 1))
    return mask


def full_kernel(tags, near, weight, gain, packed, att, lse, hidden):
    band = near.shape[1]
    cols = HEADS * HDIM
    first = first_slot(tags)
    mask = band_mask(tags, first, band)
    for j in range(MAXB):
        x = near[first + j].astype(F32)
        normed, _ = normalize(x, gain[0:1, :])
        for c in range(3):
            packed[j * band : (j + 1) * band, c * cols : (c + 1) * cols] = mm(
                normed, weight[:, c * cols : (c + 1) * cols]
            ).astype(BF16)
    own = pl.ds(pl.multiple_of((REACH - first) * band, band), band)
    queries = packed[own, 0:cols]
    lses = []
    for h in range(HEADS):
        a, b = h * HDIM, (h + 1) * HDIM
        scores = mt(queries[:, a:b], packed[:, cols + a : cols + b]) * FACTOR
        scores = jnp.where(mask, scores, MASKED)
        largest = jnp.max(scores, axis=-1, keepdims=True)
        raw = jnp.exp(scores - largest)
        summed = jnp.sum(raw, axis=-1, keepdims=True)
        probs = (raw * (1.0 / summed)).astype(BF16)
        att[:, a:b] = mm(probs, packed[:, 2 * cols + a : 2 * cols + b]).astype(BF16)
        lses.append(largest + jnp.log(summed))
    lse[...] = jnp.concatenate(lses, axis=1)
    hidden[...] = (near[REACH].astype(F32) + mt(att[...], weight[:, 3 * cols :])).astype(BF16)


def window_kernel(
    hidden_ref, cot_ref, same, weight, full_out, gain, att_full, lse_full,
    mixed, dhidden_ref, dout_full, stats, gain_row, packed, att, dpacked,
):
    cols = HEADS * HDIM
    x = hidden_ref[...].astype(F32)
    normed, inverse = normalize(x, gain[1:2, :])
    for c in range(3):
        packed[:, c * cols : (c + 1) * cols] = mm(
            normed, weight[:, c * cols : (c + 1) * cols]
        ).astype(BF16)
    cot = cot_ref[...]
    out_t = weight[:, 3 * cols :]
    dout = mm(cot, out_t).astype(BF16)
    mask = same[...] > 0.5
    for h in range(HEADS):
        a, b = h * HDIM, (h + 1) * HDIM
        q, k = packed[:, a:b], packed[:, cols + a : cols + b]
        v, g = packed[:, 2 * cols + a : 2 * cols + b], dout[:, a:b]
        scores = jnp.where(mask, mt(q, k) * FACTOR, MASKED)
        largest = jnp.max(scores, axis=-1, keepdims=True)
        raw = jnp.exp(scores - largest)
        p = raw * (1.0 / jnp.sum(raw, axis=-1, keepdims=True))
        probs = p.astype(BF16)
        out = mm(probs, v).astype(BF16)
        att[:, a:b] = out
        delta = jnp.sum(g.astype(F32) * out.astype(F32), axis=-1, keepdims=True)
        ds = (p * (mt(g, v) - delta)).astype(BF16)
        dpacked[:, a:b] = (mm(ds, k) * FACTOR).astype(BF16)
        dpacked[:, cols + a : cols + b] = (tm(ds, q) * FACTOR).astype(BF16)
        dpacked[:, 2 * cols + a : 2 * cols + b] = tm(probs, g).astype(BF16)
    mixed[...] = (x + mt(att[...], out_t)).astype(BF16)
    dnormed = mt(dpacked[...], weight[:, : 3 * cols])
    part, row = norm_back(x, gain[1:2, :], inverse, dnormed)
    gain_row[...] = row
    dhidden = cot.astype(F32) + part
    dhidden_ref[...] = dhidden
    dfull = mm(dhidden.astype(BF16), full_out[:, 3 * cols :]).astype(BF16)
    dout_full[...] = dfull
    product = dfull.astype(F32) * att_full[...].astype(F32)
    columns = [lse_full[...]] + [
        jnp.sum(product[:, h * HDIM : (h + 1) * HDIM], axis=-1, keepdims=True)
        for h in range(HEADS)
    ]
    columns.append(jnp.zeros((x.shape[0], 128 - 2 * HEADS), F32))
    stats[...] = jnp.concatenate(columns, axis=1).T[: 2 * HEADS]


def back_kernel(
    tags, packed, near_dout, near_stats, tokens, dhidden, weight, gain,
    grad_tokens, gain_row, dpacked,
):
    band = tokens.shape[0]
    cols = HEADS * HDIM
    first = first_slot(tags)
    mask = band_mask(tags, first, band)
    own = pl.ds(pl.multiple_of((REACH - first) * band, band), band)
    mine = packed[own, :]
    own_stats = near_stats[REACH].T
    gout = jnp.concatenate([near_dout[first + j] for j in range(MAXB)], axis=0)
    rows = jnp.concatenate([near_stats[first + j] for j in range(MAXB)], axis=1)
    own_out = near_dout[REACH]
    for h in range(HEADS):
        a, b = h * HDIM, (h + 1) * HDIM
        q, k, v = mine[:, a:b], mine[:, cols + a : cols + b], mine[:, 2 * cols + a : 2 * cols + b]
        g = own_out[:, a:b]
        near_q = packed[:, a:b]
        near_k = packed[:, cols + a : cols + b]
        near_v = packed[:, 2 * cols + a : 2 * cols + b]
        near_g = gout[:, a:b]
        scores = jnp.where(mask, mt(q, near_k) * FACTOR, MASKED)
        p = jnp.exp(scores - own_stats[:, h : h + 1])
        ds = (p * (mt(g, near_v) - own_stats[:, HEADS + h : HEADS + h + 1])).astype(BF16)
        dpacked[:, a:b] = (mm(ds, near_k) * FACTOR).astype(BF16)
        scores_t = jnp.where(mask, mt(k, near_q) * FACTOR - rows[h : h + 1, :], MASKED)
        pt = jnp.exp(scores_t)
        dst = (pt * (mt(v, near_g) - rows[HEADS + h : HEADS + h + 1, :])).astype(BF16)
        dpacked[:, cols + a : cols + b] = (mm(dst, near_q) * FACTOR).astype(BF16)
        dpacked[:, 2 * cols + a : 2 * cols + b] = mm(pt.astype(BF16), near_g).astype(BF16)
    dnormed = mt(dpacked[...], weight[:, : 3 * cols])
    x = tokens[...].astype(F32)
    inverse = lax.rsqrt(jnp.mean(x * x, axis=-1, keepdims=True) + EPSILON)
    part, row = norm_back(x, gain[0:1, :], inverse, dnormed)
    gain_row[...] = row
    grad_tokens[...] = dhidden[...] + part


def call(kernel, shapes, in_specs, scratch, flops, *args):
    return pl.pallas_call(
        kernel,
        out_shape=[jax.ShapeDtypeStruct(s, t) for s, t in shapes],
        in_specs=in_specs,
        out_specs=[VMEM] * len(shapes),
        scratch_shapes=scratch,
        compiler_params=pltpu.CompilerParams(vmem_limit_bytes=LIMIT),
        cost_estimate=pl.CostEstimate(flops=flops, bytes_accessed=8 << 20, transcendentals=1 << 20),
    )(*args)


def shards(tokens, cotangent, page_of_band, window_order, qkv_weight, out_weight, norm_gain):
    x = tokens[0]
    band, width = x.shape
    cols = HEADS * HDIM
    wide = 3 * cols
    weights = [
        lax.all_gather(
            jnp.concatenate([qkv_weight[i], out_weight[i].T], axis=1),
            ("enc", "dp"), axis=0, tiled=True,
        )
        for i in range(2)
    ]
    tag = jnp.broadcast_to((page_of_band + 1).astype(F32), (8, 128))
    near, near_tag = halo(0, x, tag)
    tags = near_tag[:, 0, 0].astype(jnp.int32)
    order = window_order[0, 0]
    late = jnp.arange(band)[:, None] >= WIN
    side = jnp.any((order[:, None] == jnp.arange(band)[None, :]) & late, axis=0)
    same = (side[:, None] == side[None, :]).astype(F32)
    packed, att, lse, hidden = call(
        full_kernel,
        [((MAXB * band, wide), BF16), ((band, cols), BF16), ((band, HEADS), F32), ((band, width), BF16)],
        [SMEM, VMEM, VMEM, VMEM], [], 6 << 30,
        tags, near, weights[0], norm_gain,
    )
    mixed, dhidden, dout, stats, row_window = call(
        window_kernel,
        [((band, width), BF16), ((band, width), F32), ((band, cols), BF16), ((2 * HEADS, band), F32), ((1, width), F32)],
        [VMEM] * 8,
        [pltpu.VMEM((band, wide), BF16), pltpu.VMEM((band, cols), BF16), pltpu.VMEM((band, wide), BF16)],
        3 << 30,
        hidden, cotangent[0], same, weights[1], weights[0], norm_gain, att, lse,
    )
    near_dout, near_stats = halo(1, dout, stats)
    grad_tokens, row_full = call(
        back_kernel,
        [((band, width), F32), ((1, width), F32)],
        [SMEM] + [VMEM] * 7,
        [pltpu.VMEM((band, wide), BF16)],
        3 << 30,
        tags, packed, near_dout, near_stats, x, dhidden, weights[0], norm_gain,
    )
    grad_gain = total_rows(jnp.concatenate([row_full, row_window], axis=0))
    return mixed[None], grad_tokens[None], grad_gain


def solution(mesh):
    return jax.shard_map(
        shards,
        mesh=mesh,
        in_specs=(
            P(("groups", "dp"), "enc", None),
            P(("groups", "dp"), "enc", None),
            P(("groups", "dp"), "enc"),
            P(("groups", "dp"), "enc", None),
            P(None, ("enc", "dp"), None),
            P(None, None, ("enc", "dp")),
            P(),
        ),
        out_specs=(
            P(("groups", "dp"), "enc", None),
            P(("groups", "dp"), "enc", None),
            P("groups", None),
        ),
        check_vma=False,
    )
```

time: 550 us -> 212 us (0.39); the launches traced: 541 us -> 212 us
  matrix products: 166 us -> 0 us
  starting transfers between devices: 127 us -> 0.08 us
  Pallas kernels: 0 us -> 88 us
  local copies, waits for them, and re-layouts: 89.1 us -> 7.56 us
  blocking collectives: 59.5 us -> 0 us
  waiting for transfers between devices: 71 us -> 99.6 us
  other arithmetic: 12.1 us -> 2.07 us
    dot_general x120 -> x0, matrix products: 166 us -> none  [the longest x32 32 us: head_scores(): jnp.einsum('qd,kd->qk', head_query, head_key, preferred_element_type=jnp....]
    ppermute x40 -> x0, starting transfers between devices: 127 us -> none  [shifted(): lax.ppermute(value, axis, [(source, source + steps) for source in range(f...]
    pallas_call x0 -> x6, Pallas kernels: none -> 88 us  [the longest x2 42.7 us: halo(): pl.pallas_call(functools.partial(halo_kernel, count), out_shape=[jax.Shap...]
    psum x1 -> x0, blocking collectives: 59.5 us -> none  [shards(): grad_gain = lax.psum(jnp.stack([gain_full, gain_window]), ('enc', 'dp'))]
    all_gather x4 -> x2, waiting for transfers between devices: 49.5 us -> 99.5 us  [shards(): lax.all_gather(jnp.concatenate([qkv_weight[i], out_weight[i].T], axis=1),...]
    ppermute x40 -> x0, waiting for transfers between devices: 20.8 us -> none  [shifted(): lax.ppermute(value, axis, [(source, source + steps) for source in range(f...]
    dynamic_update_slice x8 -> x0, local copies, waits for them, and re-layouts: 10.4 us -> none  [attend_forward(): lax.map(per_head, (split_heads(queries), split_heads(keys_all), split_hea...]
    transpose x5 -> x1, local copies, waits for them, and re-layouts: 10.3 us -> 0.97 us  [shards(): out_weight[i]]
  transfers between devices with their start and end apart: 44 -> 2, of which waited for: 10 -> 2; matrix products, arithmetic and copies ran while one was open for 13% -> 1% of each run, Pallas kernels for 0% -> 17%
where the time goes in v1:
time: 212 us
  waiting for transfers between devices  99.6 us (47%)
  Pallas kernels  88 us (42%)
  between operations  14.8 us (7%)
  local copies, waits for them, and re-layouts  7.56 us (4%)
    all_gather x2, waiting for transfers between devices, shards(): lax.all_gather(jnp.concatenate([qkv_weight[i], out_weight[i].T], axis=1),...  99.5 us
    pallas_call x2, Pallas kernels, halo(): pl.pallas_call(functools.partial(halo_kernel, count), out_shape=[jax.Shap...  42.7 us
    pallas_call x3, Pallas kernels, call(): pl.pallas_call(kernel, out_shape=[jax.ShapeDtypeStruct(s, t) for s, t in...  37.1 us
    pallas_call x1, Pallas kernels, total_rows(): pl.pallas_call(total_kernel, out_shape=jax.ShapeDtypeStruct(rows.shape, r...  8.2 us
    unnamed x17, local copies, waits for them, and re-layouts  5.43 us
  transfers between devices with their start and end apart: 2, of which 2 were waited for; matrix products, arithmetic and copies ran while one was open for 1% of the time, Pallas kernels for 17%

profile of v1, /device:TPU:0, one launch (start us, length us, event | category | flops | bytes accessed | tf_op | source)
XLA Modules:
  0.0 212.1 jit_solution(6256920088125385021)
XLA Ops:
  7.2 0.0 copy-start.1
  7.2 0.0 copy-start.7
  7.2 0.0 copy-start.2
  7.2 0.0 all-gather.3.cloned.1.call-start
  7.2 1.2 slice_bitcast_fusion
  8.4 1.0 slice_bitcast_fusion.2
  9.4 0.8 pad_maximum_fusion
  10.2 0.0 all-gather.3.cloned.1.call-update
  10.2 0.0 all-gather.5.cloned.1.call-start
  10.2 0.8 pad_maximum_fusion.1
  11.0 0.0 all-gather.5.cloned.1.call-update
  11.7 0.0 copy-done.1
  11.7 25.7 %shard_map.94 = (bf16[9,128,1280]{2,1,0:T(8,128)(2,1)S(1)}, f32[9,8,128]{2,1,0:T(8,128)S(1)}) custom-call(bf16[128,1280]{1,0:T(8,128)(2,1)S(1)} %bitcast.19, f32[8,128]{1,0:T(8,128)S(1)} %broadcast_in_dim.18.refs_1_), custom_call_target="tpu_custom_call" | custom-call | tf_op jit(solution)/shard_map/pallas_call | solution.py:108
  37.4 0.0 copy-start.3
  37.4 1.6 copy-done.3
  39.0 0.3 convert_reduce_fusion.tags
  39.3 0.0 copy-done.7
  39.3 0.1 fusion.1
  39.4 0.1 compare_convert_fusion.same
  39.5 49.8 %all-gather.3.cloned.1.call-done.weight.full_out = bf16[1280,2560]{1,0:T(8,128)(2,1)} async-done(((bf16[80,2560]{1,0:T(8,128)(2,1)}), bf16[1280,2560]{1,0:T(8,128)(2,1)}) %all-gather.3.cloned.1.call-update) | async-done | bytes 6553616 | tf_op jit(solution)/shard_map/all_gather | solution.py:333
  89.3 0.0 copy-done.2
  89.3 0.0 copy-start.4
  89.3 1.8 copy-done.4
  91.1 0.0 copy-start
  91.1 11.3 %shard_map.95 = (bf16[640,1920]{1,0:T(8,128)(2,1)S(1)}, bf16[128,640]{1,0:T(8,128)(2,1)S(1)}, f32[128,8]{1,0:T(8,128)S(1)}, bf16[128,1280]{1,0:T(8,128)(2,1)S(1)}) custom-call(s32[9]{0:T(128)S(1)} %convert_reduce_fusion.tags, bf16[9,128,1280]{2,1,0:T(8,128)(2,1)S(1)} %copy-done.4, bf16[1280,2560]{1,0:T(8,128)(2,1)} %all-gather.3.cloned.1.call-done.weight.full_out, ...), custom_call_target="tpu_custom_call" | custom-call | flops 6442450944 | bytes 8388608 | tf_op jit(solution)/shard_map/pallas_call | solution.py:316
  102.4 0.0 copy-start.5
  102.4 1.4 copy-done.5
  103.8 49.7 %all-gather.5.cloned.1.call-done.weight = bf16[1280,2560]{1,0:T(8,128)(2,1)} async-done(((bf16[80,2560]{1,0:T(8,128)(2,1)}), bf16[1280,2560]{1,0:T(8,128)(2,1)}) %all-gather.5.cloned.1.call-update) | async-done | bytes 6553616 | tf_op jit(solution)/shard_map/all_gather | solution.py:333
  153.6 0.0 copy-done
  153.6 0.0 copy-start.6
  153.6 15.8 %shard_map.96 = (bf16[128,1280]{1,0:T(8,128)(2,1)}, f32[128,1280]{1,0:T(8,128)S(1)}, bf16[128,640]{1,0:T(8,128)(2,1)S(1)}, f32[16,128]{1,0:T(8,128)S(1)}, f32[1,1280]{1,0:T(1,128)S(1)}) custom-call(bf16[128,1280]{1,0:T(8,128)(2,1)S(1)} %get-tuple-element.20.hidden_ref, bf16[128,1280]{1,0:T(8,128)(2,1)S(1)} %bitcast.18, ...), custom_call_target="tpu_custom_call" | custom-call | flops 3221225472 | bytes 8388608 | tf_op jit(solution)/shard_map/pallas_call | solution.py:316
  169.4 17.0 %shard_map.97 = (bf16[9,128,640]{2,1,0:T(8,128)(2,1)S(1)}, f32[9,16,128]{2,1,0:T(8,128)S(1)}) custom-call(bf16[128,640]{1,0:T(8,128)(2,1)S(1)} %get-tuple-element.25.refs_0_, f32[16,128]{1,0:T(8,128)S(1)} %get-tuple-element.26.refs_1_), custom_call_target="tpu_custom_call" | custom-call | tf_op jit(solution)/shard_map/pallas_call | solution.py:108
  186.4 0.0 copy-done.6
  186.4 10.0 %shard_map.98 = (f32[128,1280]{1,0:T(8,128)}, f32[1,1280]{1,0:T(1,128)S(1)}) custom-call(s32[9]{0:T(128)S(1)} %convert_reduce_fusion.tags, bf16[640,1920]{1,0:T(8,128)(2,1)S(1)} %copy-done.6, bf16[9,128,640]{2,1,0:T(8,128)(2,1)S(1)} %get-tuple-element.27.near_dout, f32[9,16,128]{2,1,0:T(8,128)S(1)} %get-tuple-element.28.near_stats, ...), custom_call_target="tpu_custom_call" | custom-call | flops 3221225472 | bytes 8388608 | tf_op jit(solution)/shard_map/pallas_call | solution.py:316
  196.5 8.2 %shard_map.99 = f32[2,1280]{1,0:T(2,128)S(1)} custom-call(f32[2,1280]{1,0:T(2,128)S(1)} %pad_maximum_fusion.2.row_ref), custom_call_target="tpu_custom_call" | custom-call | tf_op jit(solution)/shard_map/pallas_call | solution.py:166
  204.7 0.6 copy.12
  (3 shorter events, 0.0 us)
Async XLA Ops:
  7.2 4.5 %copy-start.1 = (bf16[1,128,1280]{2,1,0:T(8,128)(2,1)S(1)}, bf16[1,128,1280]{2,1,0:T(8,128)(2,1)}, u32[]{:S(2)}) copy-start(bf16[1,128,1280]{2,1,0:T(8,128)(2,1)} %param.7) | copy-start | bytes 983044
  7.2 32.1 %copy-start.7 = (s32[1,1,128]{2,1,0:T(1,128)S(1)}, s32[1,1,128]{2,1,0:T(1,128)}, u32[]{:S(2)}) copy-start(s32[1,1,128]{2,1,0:T(1,128)} %param.10) | copy-start | bytes 1540
  7.2 82.1 %copy-start.2 = (f32[2,1280]{1,0:T(2,128)S(1)}, f32[2,1280]{1,0:T(2,128)}, u32[]{:S(2)}) copy-start(f32[2,1280]{1,0:T(2,128)} %gain.5) | copy-start | bytes 30724
  7.2 82.1 %all-gather.3.cloned.1.call-start = ((), (), s32[]{:S(2)}) async-start(), calls=%async_computation | async-start | bytes 6963200 | tf_op jit(solution)/shard_map/all_gather | solution.py:333
  10.2 143.4 %all-gather.5.cloned.1.call-start = ((), (), s32[]{:S(2)}) async-start(), calls=%async_computation.1 | async-start | bytes 6963200 | tf_op jit(solution)/shard_map/all_gather | solution.py:333
  37.4 1.6 copy-start.3
  89.3 1.8 copy-start.4
  91.1 62.4 %copy-start = (bf16[1,128,1280]{2,1,0:T(8,128)(2,1)S(1)}, bf16[1,128,1280]{2,1,0:T(8,128)(2,1)}, u32[]{:S(2)}) copy-start(bf16[1,128,1280]{2,1,0:T(8,128)(2,1)} %param.8) | copy-start | bytes 983044
  102.4 1.4 copy-start.5
  153.6 32.9 %copy-start.6 = (bf16[640,1920]{1,0:T(8,128)(2,1)S(1)}, bf16[640,1920]{1,0:T(8,128)(2,1)}, u32[]{:S(2)}) copy-start(bf16[640,1920]{1,0:T(8,128)(2,1)} %copy-done.5) | copy-start | bytes 7372804
Sparse Core Ops, SparseCore 0:
  10.9 78.3 all-gather.2
  91.6 61.9 all-gather.4

commit v2 on v1

--- a/solution.py
+++ b/solution.py
@@ -118,6 +118,165 @@
             collective_id=collective_id, has_side_effects=True, vmem_limit_bytes=LIMIT
         ),
     )(*arrays)
+
+
+def gather_halo_kernel(count, *refs):
+    n = lax.axis_size("enc")
+    weight, ins, full, outs = refs[0], refs[1 : 1 + count], refs[1 + count], refs[2 + count : 2 + 2 * count]
+    send, recv, shard_send, shard_recv = refs[2 + 2 * count :]
+    me = lax.axis_index("enc")
+    barrier = pltpu.get_barrier_semaphore()
+    planes = n // 4
+    z = me // 4
+    across = me + 2 - 4 * (lax.rem(me, 4) // 2)
+    other = me + 1 - 2 * lax.rem(me, 2)
+
+    def valid(d):
+        return me + d < n if d > 0 else me + d >= 0
+
+    def copy(a, d, source, slot):
+        return pltpu.make_async_remote_copy(
+            src_ref=source,
+            dst_ref=outs[a].at[slot],
+            send_sem=send.at[a, REACH + d],
+            recv_sem=recv.at[a, slot],
+            device_id={"enc": me + d},
+            device_id_type=MESH,
+        )
+
+    def shard(s, to, k, source=None):
+        return pltpu.make_async_remote_copy(
+            src_ref=full.at[s] if source is None else source,
+            dst_ref=full.at[s],
+            send_sem=shard_send.at[s, k],
+            recv_sem=shard_recv.at[s],
+            device_id={"enc": to},
+            device_id_type=MESH,
+        )
+
+    for d in OFFSETS:
+
+        @pl.when(valid(d))
+        def _():
+            pl.semaphore_signal(barrier, inc=1, device_id={"enc": me + d}, device_id_type=MESH)
+
+    pl.semaphore_wait(barrier, jnp.minimum(me, REACH) + jnp.minimum(n - 1 - me, REACH))
+
+    @pl.when(z + 1 < planes)
+    def _():
+        shard(me, me + 4, 0, weight).start()
+
+    @pl.when(z > 0)
+    def _():
+        shard(me, me - 4, 1, weight).start()
+
+    shard(me, across, 2, weight).start()
+    shard(me, other, 3, weight).start()
+    for d in OFFSETS:
+
+        @pl.when(valid(d))
+        def _():
+            for a in range(count):
+                copy(a, d, ins[a], REACH - d).start()
+
+    full[me] = weight[...]
+    for a in range(count):
+        outs[a][REACH] = ins[a][...]
+    for d in OFFSETS:
+
+        @pl.when(jnp.logical_not(valid(d)))
+        def _():
+            for a in range(count):
+                outs[a][REACH + d] = jnp.zeros(ins[a].shape, ins[a].dtype)
+
+    def present(step):
+        return z + step < planes if step > 0 else z + step >= 0
+
+    for distance in range(1, planes + 1):
+        if distance < planes:
+            for step in (-distance, distance):
+
+                @pl.when(present(step))
+                def _():
+                    s = me + 4 * step
+                    shard(s, other, 3).wait_recv()
+                    back = -1 if step > 0 else 1
+
+                    @pl.when(present(back))
+                    def _():
+                        shard(s, me + 4 * back, 0).start()
+
+                    shard(s, across, 2).start()
+                    shard(s, other, 3).start()
+
+        for step in sorted({1 - distance, distance - 1}):
+
+            @pl.when(present(step))
+            def _():
+                s = across + 4 * step
+                shard(s, other, 3).wait_recv()
+                shard(s, other, 3).start()
+
+    for plane in range(planes):
+        for x in range(2):
+            s = 4 * plane + 2 * x + lax.rem(other, 2)
+            shard(s, other, 3).wait_recv()
+
+    for d in OFFSETS:
+
+        @pl.when(valid(d))
+        def _():
+            for a in range(count):
+                copy(a, d, ins[a], REACH - d).wait_send()
+                copy(a, d, ins[a], REACH + d).wait_recv()
+
+    @pl.when(z + 1 < planes)
+    def _():
+        shard(me, me + 4, 0, weight).wait_send()
+
+    @pl.when(z > 0)
+    def _():
+        shard(me, me - 4, 1, weight).wait_send()
+
+    shard(me, across, 2, weight).wait_send()
+    shard(me, other, 3, weight).wait_send()
+    for distance in range(planes):
+        for step in sorted({-distance, distance}):
+
+            @pl.when(present(step))
+            def _():
+                s = me + 4 * step
+                if distance > 0:
+                    back = -1 if step > 0 else 1
+
+                    @pl.when(present(back))
+                    def _():
+                        shard(s, me + 4 * back, 0).wait_send()
+
+                    shard(s, across, 2).wait_send()
+                    shard(s, other, 3).wait_send()
+                shard(across + 4 * step, other, 3).wait_send()
+
+
+def gather_halo(weight, *arrays):
+    count = len(arrays)
+    n = lax.axis_size("enc")
+    return pl.pallas_call(
+        functools.partial(gather_halo_kernel, count),
+        out_shape=[jax.ShapeDtypeStruct((n,) + weight.shape, weight.dtype)]
+        + [jax.ShapeDtypeStruct((SLOTS,) + a.shape, a.dtype) for a in arrays],
+        in_specs=[VMEM] * (count + 1),
+        out_specs=[VMEM] * (count + 1),
+        scratch_shapes=[
+            pltpu.SemaphoreType.DMA((count, SLOTS)),
+            pltpu.SemaphoreType.DMA((count, SLOTS)),
+            pltpu.SemaphoreType.DMA((n, 4)),
+            pltpu.SemaphoreType.DMA((n,)),
+        ],
+        compiler_params=pltpu.CompilerParams(
+            collective_id=0, has_side_effects=True, vmem_limit_bytes=LIMIT
+        ),
+    )(weight, *arrays)
 
 
 def total_kernel(row_ref, out_ref, held, send, recv):
@@ -329,15 +488,18 @@
     band, width = x.shape
     cols = HEADS * HDIM
     wide = 3 * cols
+    pieces = [jnp.concatenate([qkv_weight[i], out_weight[i].T], axis=1) for i in range(2)]
+    tag = jnp.broadcast_to((page_of_band + 1).astype(F32), (8, 128))
+    gathers = lax.axis_size("dp") == 1 and lax.axis_size("enc") % 4 == 0 and pieces[0].shape[0] % 16 == 0
     weights = [
-        lax.all_gather(
-            jnp.concatenate([qkv_weight[i], out_weight[i].T], axis=1),
-            ("enc", "dp"), axis=0, tiled=True,
-        )
+        None if gathers and i == 0 else lax.all_gather(pieces[i], ("enc", "dp"), axis=0, tiled=True)
         for i in range(2)
     ]
-    tag = jnp.broadcast_to((page_of_band + 1).astype(F32), (8, 128))
-    near, near_tag = halo(0, x, tag)
+    if gathers:
+        full, near, near_tag = gather_halo(pieces[0], x, tag)
+        weights[0] = full.reshape(width, pieces[0].shape[1])
+    else:
+        near, near_tag = halo(0, x, tag)
     tags = near_tag[:, 0, 0].astype(jnp.int32)
     order = window_order[0, 0]
     late = jnp.arange(band)[:, None] >= WIN

time: 212 us -> 183 us (0.86)
  waiting for transfers between devices: 99.6 us -> 0.02 us
  Pallas kernels: 88 us -> 163 us
  local copies, waits for them, and re-layouts: 7.56 us -> 4.16 us
    all_gather x2 -> x1, waiting for transfers between devices: 99.5 us -> 0.01 us  [shards(): lax.all_gather(pieces[i], ('enc', 'dp'), axis=0, tiled=True)]
    pallas_call x0 -> x1, Pallas kernels: none -> 97.7 us  [gather_halo(): pl.pallas_call(functools.partial(gather_halo_kernel, count), out_shape=[j...]
    pallas_call x2 -> x1, Pallas kernels: 42.7 us -> 19.8 us  [halo(): pl.pallas_call(functools.partial(halo_kernel, count), out_shape=[jax.Shap...]
    unnamed x17 -> x13, local copies, waits for them, and re-layouts: 5.43 us -> 2.03 us
  transfers between devices with their start and end apart: 2 -> 1, of which waited for: 2 -> 0; matrix products, arithmetic and copies ran while one was open for 1% -> 0% of each run, Pallas kernels for 17% -> 60%
where the time goes in v2:
time: 183 us
  Pallas kernels  163 us (89%)
  between operations  14.8 us (8%)
  local copies, waits for them, and re-layouts  4.16 us (2%)
    pallas_call x1, Pallas kernels, gather_halo(): pl.pallas_call(functools.partial(gather_halo_kernel, count), out_shape=[j...  97.7 us
    pallas_call x3, Pallas kernels, call(): pl.pallas_call(kernel, out_shape=[jax.ShapeDtypeStruct(s, t) for s, t in...  37.2 us
    pallas_call x1, Pallas kernels, halo(): pl.pallas_call(functools.partial(halo_kernel, count), out_shape=[jax.Shap...  19.8 us
    pallas_call x1, Pallas kernels, total_rows(): pl.pallas_call(total_kernel, out_shape=jax.ShapeDtypeStruct(rows.shape, r...  8.19 us
  transfers between devices with their start and end apart: 1, of which 0 were waited for; matrix products, arithmetic and copies ran while one was open for 0% of the time, Pallas kernels for 60%

profile of v2, /device:TPU:0, one launch (start us, length us, event | category | flops | bytes accessed | tf_op | source)
XLA Modules:
  0.0 183.1 jit_solution(17663244801142948311)
XLA Ops:
  7.2 0.0 copy-start.1
  7.2 0.0 copy-start.5
  7.2 0.0 copy-start.2
  7.2 0.0 all-gather.2.cloned.1.call-start
  7.2 1.2 slice_bitcast_fusion
  8.4 1.0 slice_bitcast_fusion.2
  9.4 0.8 pad_maximum_fusion.1
  10.2 0.0 all-gather.2.cloned.1.call-update
  10.9 0.0 copy-done.1
  10.9 97.7 %shard_map.94 = (bf16[16,80,2560]{2,1,0:T(8,128)(2,1)}, bf16[9,128,1280]{2,1,0:T(8,128)(2,1)S(1)}, f32[9,8,128]{2,1,0:T(8,128)S(1)}) custom-call(bf16[80,2560]{1,0:T(8,128)(2,1)S(1)} %pad_maximum_fusion.refs_0_, bf16[128,1280]{1,0:T(8,128)(2,1)S(1)} %bitcast.20, f32[8,128]{1,0:T(8,128)S(1)} %broadcast_in_dim.18.refs_2_), custom_call_target="tpu_custom_call" | custom-call | tf_op jit(solution)/shard_map/pallas_call | solution.py:264
  108.6 0.3 convert_reduce_fusion.tags
  108.8 0.0 copy-done.5
  108.8 0.1 fusion.1
  109.0 0.1 compare_convert_fusion.same
  109.0 0.0 copy-done.2
  109.1 0.0 copy-start
  109.1 11.4 %shard_map.95 = (bf16[640,1920]{1,0:T(8,128)(2,1)S(1)}, bf16[128,640]{1,0:T(8,128)(2,1)S(1)}, f32[128,8]{1,0:T(8,128)S(1)}, bf16[128,1280]{1,0:T(8,128)(2,1)S(1)}) custom-call(s32[9]{0:T(128)S(1)} %convert_reduce_fusion.tags, bf16[9,128,1280]{2,1,0:T(8,128)(2,1)S(1)} %get-tuple-element.20.near, bf16[1280,2560]{1,0:T(8,128)(2,1)} %bitcast.22, ...), custom_call_target="tpu_custom_call" | custom-call | flops 6442450944 | bytes 8388608 | tf_op jit(solution)/shard_map/pallas_call | solution.py:475
  120.4 0.0 copy-start.3
  120.5 1.4 copy-done.3
  121.9 0.0 all-gather.2.cloned.1.call-done.weight
  121.9 0.0 copy-done
  121.9 0.0 copy-start.4
  121.9 15.8 %shard_map.96 = (bf16[128,1280]{1,0:T(8,128)(2,1)}, f32[128,1280]{1,0:T(8,128)S(1)}, bf16[128,640]{1,0:T(8,128)(2,1)S(1)}, f32[16,128]{1,0:T(8,128)S(1)}, f32[1,1280]{1,0:T(1,128)S(1)}) custom-call(bf16[128,1280]{1,0:T(8,128)(2,1)S(1)} %get-tuple-element.22.hidden_ref, bf16[128,1280]{1,0:T(8,128)(2,1)S(1)} %bitcast.19, ...), custom_call_target="tpu_custom_call" | custom-call | flops 3221225472 | bytes 8388608 | tf_op jit(solution)/shard_map/pallas_call | solution.py:475
  137.7 19.8 %shard_map.97 = (bf16[9,128,640]{2,1,0:T(8,128)(2,1)S(1)}, f32[9,16,128]{2,1,0:T(8,128)S(1)}) custom-call(bf16[128,640]{1,0:T(8,128)(2,1)S(1)} %get-tuple-element.27.refs_0_, f32[16,128]{1,0:T(8,128)S(1)} %get-tuple-element.28.refs_1_), custom_call_target="tpu_custom_call" | custom-call | tf_op jit(solution)/shard_map/pallas_call | solution.py:108
  157.4 0.0 copy-done.4
  157.5 10.0 %shard_map.98 = (f32[128,1280]{1,0:T(8,128)}, f32[1,1280]{1,0:T(1,128)S(1)}) custom-call(s32[9]{0:T(128)S(1)} %convert_reduce_fusion.tags, bf16[640,1920]{1,0:T(8,128)(2,1)S(1)} %copy-done.4, bf16[9,128,640]{2,1,0:T(8,128)(2,1)S(1)} %get-tuple-element.29.near_dout, f32[9,16,128]{2,1,0:T(8,128)S(1)} %get-tuple-element.30.near_stats, ...), custom_call_target="tpu_custom_call" | custom-call | flops 3221225472 | bytes 8388608 | tf_op jit(solution)/shard_map/pallas_call | solution.py:475
  167.5 8.2 %shard_map.99 = f32[2,1280]{1,0:T(2,128)S(1)} custom-call(f32[2,1280]{1,0:T(2,128)S(1)} %pad_maximum_fusion.2.row_ref), custom_call_target="tpu_custom_call" | custom-call | tf_op jit(solution)/shard_map/pallas_call | solution.py:325
  175.7 0.6 copy.12
  (4 shorter events, 0.1 us)
Async XLA Ops:
  7.2 3.7 %copy-start.1 = (bf16[1,128,1280]{2,1,0:T(8,128)(2,1)S(1)}, bf16[1,128,1280]{2,1,0:T(8,128)(2,1)}, u32[]{:S(2)}) copy-start(bf16[1,128,1280]{2,1,0:T(8,128)(2,1)} %param.7) | copy-start | bytes 983044
  7.2 101.7 %copy-start.5 = (s32[1,1,128]{2,1,0:T(1,128)S(1)}, s32[1,1,128]{2,1,0:T(1,128)}, u32[]{:S(2)}) copy-start(s32[1,1,128]{2,1,0:T(1,128)} %param.10) | copy-start | bytes 1540
  7.2 101.9 %copy-start.2 = (f32[2,1280]{1,0:T(2,128)S(1)}, f32[2,1280]{1,0:T(2,128)}, u32[]{:S(2)}) copy-start(f32[2,1280]{1,0:T(2,128)} %gain.5) | copy-start | bytes 30724
  7.2 114.7 %all-gather.2.cloned.1.call-start = ((), (), s32[]{:S(2)}) async-start(), calls=%async_computation | async-start | bytes 6963200 | tf_op jit(solution)/shard_map/all_gather | solution.py:495
  109.1 12.8 %copy-start = (bf16[1,128,1280]{2,1,0:T(8,128)(2,1)S(1)}, bf16[1,128,1280]{2,1,0:T(8,128)(2,1)}, u32[]{:S(2)}) copy-start(bf16[1,128,1280]{2,1,0:T(8,128)(2,1)} %param.8) | copy-start | bytes 983044
  120.4 1.4 copy-start.3
  121.9 35.6 %copy-start.4 = (bf16[640,1920]{1,0:T(8,128)(2,1)S(1)}, bf16[640,1920]{1,0:T(8,128)(2,1)}, u32[]{:S(2)}) copy-start(bf16[640,1920]{1,0:T(8,128)(2,1)} %copy-done.3) | copy-start | bytes 7372804
Sparse Core Ops, SparseCore 0:
  10.9 100.4 all-gather.1

commit v3 on v1

--- a/solution.py
+++ b/solution.py
@@ -118,6 +118,171 @@
             collective_id=collective_id, has_side_effects=True, vmem_limit_bytes=LIMIT
         ),
     )(*arrays)
+
+
+def gather_halo_kernel(count, *refs):
+    n = lax.axis_size("enc")
+    pieces, ins, fulls = refs[:2], refs[2 : 2 + count], refs[2 + count : 4 + count]
+    outs = refs[4 + count : 4 + 2 * count]
+    send, recv, shard_send, shard_recv = refs[4 + 2 * count :]
+    me, group = lax.axis_index("enc"), lax.axis_index("groups")
+    half = pieces[0].shape[1] // 2
+    barrier = pltpu.get_barrier_semaphore()
+    planes = n // 4
+    z = me // 4
+    across = me + 2 - 4 * (lax.rem(me, 4) // 2)
+    other = me + 1 - 2 * lax.rem(me, 2)
+    sent = []
+
+    def valid(d):
+        return me + d < n if d > 0 else me + d >= 0
+
+    def present(*steps):
+        good = z >= 0
+        for step in steps:
+            good = jnp.logical_and(good, z + step < planes if step > 0 else z + step >= 0)
+        return good
+
+    def copy(a, d, source, slot):
+        return pltpu.make_async_remote_copy(
+            src_ref=source,
+            dst_ref=outs[a].at[slot],
+            send_sem=send.at[a, REACH + d],
+            recv_sem=recv.at[a, slot],
+            device_id={"enc": me + d},
+            device_id_type=MESH,
+        )
+
+    def shard(s, part, k, device, source=None):
+        if part is None:
+            dst, unit = fulls[0].at[s], 0
+        else:
+            columns = pl.ds(pl.multiple_of(part * half, half), half)
+            dst, unit = fulls[1].at[s, :, columns], 1 + part
+            if source is not None:
+                source = source.at[:, columns]
+        return pltpu.make_async_remote_copy(
+            src_ref=dst if source is None else source,
+            dst_ref=dst,
+            send_sem=shard_send.at[s, unit, k],
+            recv_sem=shard_recv.at[s, unit],
+            device_id=device,
+            device_id_type=MESH,
+        )
+
+    core, side, twin = {"enc": other}, {"enc": across}, {"groups": 1 - group}
+
+    def begin(steps, s, part, k, device, source=None):
+        sent.append((steps, s, part, k, device, source))
+
+        @pl.when(present(*steps))
+        def _():
+            shard(s, part, k, device, source).start()
+
+    def arrive(steps, s, part):
+        @pl.when(present(*steps))
+        def _():
+            shard(s, part, 3, core).wait_recv()
+
+    for d in OFFSETS:
+
+        @pl.when(valid(d))
+        def _():
+            pl.semaphore_signal(barrier, inc=1, device_id={"enc": me + d}, device_id_type=MESH)
+
+    pl.semaphore_signal(barrier, inc=1, device_id=twin, device_id_type=MESH)
+    pl.semaphore_wait(barrier, jnp.minimum(me, REACH) + jnp.minimum(n - 1 - me, REACH) + 1)
+
+    for part, piece in ((None, pieces[0]), (group, pieces[1])):
+        begin((1,), me, part, 0, {"enc": me + 4}, piece)
+        begin((-1,), me, part, 1, {"enc": me - 4}, piece)
+        begin((), me, part, 2, side, piece)
+        begin((), me, part, 3, core, piece)
+    begin((), me, 1 - group, 3, core, pieces[1])
+    for d in OFFSETS:
+
+        @pl.when(valid(d))
+        def _():
+            for a in range(count):
+                copy(a, d, ins[a], REACH - d).start()
+
+    for f in range(2):
+        fulls[f][me] = pieces[f][...]
+    for a in range(count):
+        outs[a][REACH] = ins[a][...]
+    for d in OFFSETS:
+
+        @pl.when(jnp.logical_not(valid(d)))
+        def _():
+            for a in range(count):
+                outs[a][REACH + d] = jnp.zeros(ins[a].shape, ins[a].dtype)
+
+    def steps_at(distance):
+        return sorted({-distance, distance}) if 0 <= distance < planes else []
+
+    for distance in range(1, planes + 2):
+        for part in (None, group):
+            for step in steps_at(distance):
+                s, back = me + 4 * step, -1 if step > 0 else 1
+                arrive((step,), s, part)
+                begin((step, back), s, part, 0, {"enc": me + 4 * back})
+                begin((step,), s, part, 2, side)
+                begin((step,), s, part, 3, core)
+                if part is not None:
+                    begin((step,), s, part, 4, twin)
+        for part in (None, group):
+            for step in steps_at(distance - 1):
+                s = across + 4 * step
+                arrive((step,), s, part)
+                begin((step,), s, part, 3, core)
+                if part is not None:
+                    begin((step,), s, part, 4, twin)
+        lines = [(step, me + 4 * step) for step in steps_at(distance - 1) if step]
+        lines += [(step, across + 4 * step) for step in steps_at(distance - 2)]
+        for step, s in lines:
+            arrive((step,), s, 1 - group)
+            begin((step,), s, 1 - group, 3, core)
+
+    for plane in range(planes):
+        for x in range(2):
+            s = 4 * plane + 2 * x + lax.rem(other, 2)
+            for part in (None, 0, 1):
+                arrive((), s, part)
+
+    for d in OFFSETS:
+
+        @pl.when(valid(d))
+        def _():
+            for a in range(count):
+                copy(a, d, ins[a], REACH - d).wait_send()
+                copy(a, d, ins[a], REACH + d).wait_recv()
+
+    for steps, *rest in sent:
+
+        @pl.when(present(*steps))
+        def _():
+            shard(*rest).wait_send()
+
+
+def gather_halo(pieces, *arrays):
+    count = len(arrays)
+    n = lax.axis_size("enc")
+    return pl.pallas_call(
+        functools.partial(gather_halo_kernel, count),
+        out_shape=[jax.ShapeDtypeStruct((n,) + p.shape, p.dtype) for p in pieces]
+        + [jax.ShapeDtypeStruct((SLOTS,) + a.shape, a.dtype) for a in arrays],
+        in_specs=[VMEM] * (count + 2),
+        out_specs=[VMEM] * (count + 2),
+        scratch_shapes=[
+            pltpu.SemaphoreType.DMA((count, SLOTS)),
+            pltpu.SemaphoreType.DMA((count, SLOTS)),
+            pltpu.SemaphoreType.DMA((n, 3, 5)),
+            pltpu.SemaphoreType.DMA((n, 3)),
+        ],
+        compiler_params=pltpu.CompilerParams(
+            collective_id=0, has_side_effects=True, vmem_limit_bytes=LIMIT
+        ),
+    )(*pieces, *arrays)
 
 
 def total_kernel(row_ref, out_ref, held, send, recv):
@@ -329,15 +494,16 @@
     band, width = x.shape
     cols = HEADS * HDIM
     wide = 3 * cols
-    weights = [
-        lax.all_gather(
-            jnp.concatenate([qkv_weight[i], out_weight[i].T], axis=1),
-            ("enc", "dp"), axis=0, tiled=True,
-        )
-        for i in range(2)
-    ]
+    pieces = [jnp.concatenate([qkv_weight[i], out_weight[i].T], axis=1) for i in range(2)]
     tag = jnp.broadcast_to((page_of_band + 1).astype(F32), (8, 128))
-    near, near_tag = halo(0, x, tag)
+    gathers = lax.axis_size("dp") == 1 and lax.axis_size("groups") == 2
+    gathers = gathers and lax.axis_size("enc") % 4 == 0 and pieces[0].shape[0] % 16 == 0
+    if gathers:
+        *fulls, near, near_tag = gather_halo(pieces, x, tag)
+        weights = [full.reshape(width, full.shape[2]) for full in fulls]
+    else:
+        weights = [lax.all_gather(p, ("enc", "dp"), axis=0, tiled=True) for p in pieces]
+        near, near_tag = halo(0, x, tag)
     tags = near_tag[:, 0, 0].astype(jnp.int32)
     order = window_order[0, 0]
     late = jnp.arange(band)[:, None] >= WIN

time: 212 us -> 170 us (0.80)
  waiting for transfers between devices: 99.6 us -> 0 us
  Pallas kernels: 88 us -> 165 us
  between operations: 14.8 us -> 1.42 us
  local copies, waits for them, and re-layouts: 7.56 us -> 2.74 us
    all_gather x2 -> x0, waiting for transfers between devices: 99.5 us -> none  [shards(): lax.all_gather(jnp.concatenate([qkv_weight[i], out_weight[i].T], axis=1),...]
    pallas_call x0 -> x1, Pallas kernels: none -> 92.3 us  [gather_halo(): pl.pallas_call(functools.partial(gather_halo_kernel, count), out_shape=[j...]
    pallas_call x2 -> x1, Pallas kernels: 42.7 us -> 26.7 us  [halo(): pl.pallas_call(functools.partial(halo_kernel, count), out_shape=[jax.Shap...]
    unnamed x17 -> x9, local copies, waits for them, and re-layouts: 5.43 us -> 0.62 us
  transfers between devices with their start and end apart: 2 -> 0, of which waited for: 2 -> 0; matrix products, arithmetic and copies ran while one was open for 1% -> 0% of each run, Pallas kernels for 17% -> 0%
where the time goes in v3:
time: 170 us; the launch traced here: 169 us
  Pallas kernels  165 us (97%)
  local copies, waits for them, and re-layouts  2.74 us (2%)
    pallas_call x1, Pallas kernels, gather_halo(): pl.pallas_call(functools.partial(gather_halo_kernel, count), out_shape=[j...  92.3 us
    pallas_call x3, Pallas kernels, call(): pl.pallas_call(kernel, out_shape=[jax.ShapeDtypeStruct(s, t) for s, t in...  36.9 us
    pallas_call x1, Pallas kernels, halo(): pl.pallas_call(functools.partial(halo_kernel, count), out_shape=[jax.Shap...  26.7 us
    pallas_call x1, Pallas kernels, total_rows(): pl.pallas_call(total_kernel, out_shape=jax.ShapeDtypeStruct(rows.shape, r...  8.63 us

profile of v3, /device:TPU:0, one launch (start us, length us, event | category | flops | bytes accessed | tf_op | source)
XLA Modules:
  0.0 169.3 jit_solution(201606087126692391)
XLA Ops:
  0.6 0.0 copy-start.1
  0.6 0.0 copy-start.2
  0.7 1.1 slice_bitcast_fusion
  1.8 1.0 slice_bitcast_fusion.2
  2.8 0.1 pad_maximum_fusion
  3.5 0.0 copy-done.1
  3.5 92.3 %shard_map.94 = (bf16[16,80,2560]{2,1,0:T(8,128)(2,1)}, bf16[16,80,2560]{2,1,0:T(8,128)(2,1)}, bf16[9,128,1280]{2,1,0:T(8,128)(2,1)S(1)}, f32[9,8,128]{2,1,0:T(8,128)S(1)}) custom-call(bf16[80,2560]{1,0:T(8,128)(2,1)S(1)} %get-tuple-element.41.refs_0_, bf16[80,2560]{1,0:T(8,128)(2,1)S(1)} %get-tuple-element.42.refs_1_, bf16[128,1280]{1,0:T(8,128)(2,1)S(1)} %bitcast.21, ...), custom_call_target="tpu_custom_call" | custom-call | tf_op jit(solution)/shard_map/pallas_call | solution.py:270
  95.8 0.3 convert_reduce_fusion.tags
  96.1 0.0 copy-done.2
  96.1 0.0 copy-start.3
  96.1 0.0 copy-start
  96.1 11.3 %shard_map.95 = (bf16[640,1920]{1,0:T(8,128)(2,1)S(1)}, bf16[128,640]{1,0:T(8,128)(2,1)S(1)}, f32[128,8]{1,0:T(8,128)S(1)}, bf16[128,1280]{1,0:T(8,128)(2,1)S(1)}) custom-call(s32[9]{0:T(128)S(1)} %convert_reduce_fusion.tags, bf16[9,128,1280]{2,1,0:T(8,128)(2,1)S(1)} %get-tuple-element.21.near, bf16[1280,2560]{1,0:T(8,128)(2,1)} %bitcast.23, ...), custom_call_target="tpu_custom_call" | custom-call | flops 6442450944 | bytes 8388608 | tf_op jit(solution)/shard_map/pallas_call | solution.py:481
  107.4 0.0 copy-done.3
  107.4 0.1 fusion.1
  107.5 0.1 compare_convert_fusion.same
  107.6 0.0 copy-done
  107.7 15.6 %shard_map.96 = (bf16[128,1280]{1,0:T(8,128)(2,1)}, f32[128,1280]{1,0:T(8,128)S(1)}, bf16[128,640]{1,0:T(8,128)(2,1)S(1)}, f32[16,128]{1,0:T(8,128)S(1)}, f32[1,1280]{1,0:T(1,128)S(1)}) custom-call(bf16[128,1280]{1,0:T(8,128)(2,1)S(1)} %get-tuple-element.23.hidden_ref, bf16[128,1280]{1,0:T(8,128)(2,1)S(1)} %bitcast.20, ...), custom_call_target="tpu_custom_call" | custom-call | flops 3221225472 | bytes 8388608 | tf_op jit(solution)/shard_map/pallas_call | solution.py:481
  123.3 26.7 %shard_map.97 = (bf16[9,128,640]{2,1,0:T(8,128)(2,1)S(1)}, f32[9,16,128]{2,1,0:T(8,128)S(1)}) custom-call(bf16[128,640]{1,0:T(8,128)(2,1)S(1)} %get-tuple-element.29.refs_0_, f32[16,128]{1,0:T(8,128)S(1)} %get-tuple-element.30.refs_1_), custom_call_target="tpu_custom_call" | custom-call | tf_op jit(solution)/shard_map/pallas_call | solution.py:108
  150.1 10.0 %shard_map.98 = (f32[128,1280]{1,0:T(8,128)}, f32[1,1280]{1,0:T(1,128)S(1)}) custom-call(s32[9]{0:T(128)S(1)} %convert_reduce_fusion.tags, bf16[640,1920]{1,0:T(8,128)(2,1)S(1)} %get-tuple-element.28.packed, bf16[9,128,640]{2,1,0:T(8,128)(2,1)S(1)} %get-tuple-element.31.near_dout, f32[9,16,128]{2,1,0:T(8,128)S(1)} %get-tuple-element.32.near_stats, ...), custom_call_target="tpu_custom_call" | custom-call | flops 3221225472 | bytes 8388608 | tf_op jit(solution)/shard_map/pallas_call | solution.py:481
  160.1 8.6 %shard_map.99 = f32[2,1280]{1,0:T(2,128)S(1)} custom-call(f32[2,1280]{1,0:T(2,128)S(1)} %pad_maximum_fusion.2.row_ref), custom_call_target="tpu_custom_call" | custom-call | tf_op jit(solution)/shard_map/pallas_call | solution.py:331
  168.7 0.6 copy.12
  (3 shorter events, 0.0 us)
Async XLA Ops:
  0.6 2.9 %copy-start.1 = (bf16[1,128,1280]{2,1,0:T(8,128)(2,1)S(1)}, bf16[1,128,1280]{2,1,0:T(8,128)(2,1)}, u32[]{:S(2)}) copy-start(bf16[1,128,1280]{2,1,0:T(8,128)(2,1)} %param.7) | copy-start | bytes 983044
  0.6 95.5 %copy-start.2 = (f32[2,1280]{1,0:T(2,128)S(1)}, f32[2,1280]{1,0:T(2,128)}, u32[]{:S(2)}) copy-start(f32[2,1280]{1,0:T(2,128)} %gain.5) | copy-start | bytes 30724
  96.1 11.3 %copy-start.3 = (s32[1,1,128]{2,1,0:T(1,128)S(1)}, s32[1,1,128]{2,1,0:T(1,128)}, u32[]{:S(2)}) copy-start(s32[1,1,128]{2,1,0:T(1,128)} %param.10) | copy-start | bytes 1540
  96.1 11.5 %copy-start = (bf16[1,128,1280]{2,1,0:T(8,128)(2,1)S(1)}, bf16[1,128,1280]{2,1,0:T(8,128)(2,1)}, u32[]{:S(2)}) copy-start(bf16[1,128,1280]{2,1,0:T(8,128)(2,1)} %param.8) | copy-start | bytes 983044

commit v4 on v3

--- a/solution.py
+++ b/solution.py
@@ -154,13 +154,11 @@
         )
 
     def shard(s, part, k, device, source=None):
-        if part is None:
-            dst, unit = fulls[0].at[s], 0
-        else:
-            columns = pl.ds(pl.multiple_of(part * half, half), half)
-            dst, unit = fulls[1].at[s, :, columns], 1 + part
-            if source is not None:
-                source = source.at[:, columns]
+        layer, piece = part
+        columns = pl.ds(pl.multiple_of(piece * half, half), half)
+        dst, unit = fulls[layer].at[s, :, columns], 2 * layer + piece
+        if source is not None:
+            source = source.at[:, columns]
         return pltpu.make_async_remote_copy(
             src_ref=dst if source is None else source,
             dst_ref=dst,
@@ -193,12 +191,13 @@
     pl.semaphore_signal(barrier, inc=1, device_id=twin, device_id_type=MESH)
     pl.semaphore_wait(barrier, jnp.minimum(me, REACH) + jnp.minimum(n - 1 - me, REACH) + 1)
 
-    for part, piece in ((None, pieces[0]), (group, pieces[1])):
+    for layer, piece in enumerate(pieces):
+        part = (layer, group)
         begin((1,), me, part, 0, {"enc": me + 4}, piece)
         begin((-1,), me, part, 1, {"enc": me - 4}, piece)
         begin((), me, part, 2, side, piece)
         begin((), me, part, 3, core, piece)
-    begin((), me, 1 - group, 3, core, pieces[1])
+        begin((), me, (layer, 1 - group), 3, core, piece)
     for d in OFFSETS:
 
         @pl.when(valid(d))
@@ -221,32 +220,31 @@
         return sorted({-distance, distance}) if 0 <= distance < planes else []
 
     for distance in range(1, planes + 2):
-        for part in (None, group):
+        for part in ((0, group), (1, group)):
             for step in steps_at(distance):
                 s, back = me + 4 * step, -1 if step > 0 else 1
                 arrive((step,), s, part)
                 begin((step, back), s, part, 0, {"enc": me + 4 * back})
                 begin((step,), s, part, 2, side)
                 begin((step,), s, part, 3, core)
-                if part is not None:
-                    begin((step,), s, part, 4, twin)
-        for part in (None, group):
+                begin((step,), s, part, 4, twin)
+        for part in ((0, group), (1, group)):
             for step in steps_at(distance - 1):
                 s = across + 4 * step
                 arrive((step,), s, part)
                 begin((step,), s, part, 3, core)
-                if part is not None:
-                    begin((step,), s, part, 4, twin)
+                begin((step,), s, part, 4, twin)
         lines = [(step, me + 4 * step) for step in steps_at(distance - 1) if step]
         lines += [(step, across + 4 * step) for step in steps_at(distance - 2)]
-        for step, s in lines:
-            arrive((step,), s, 1 - group)
-            begin((step,), s, 1 - group, 3, core)
+        for layer in range(2):
+            for step, s in lines:
+                arrive((step,), s, (layer, 1 - group))
+                begin((step,), s, (layer, 1 - group), 3, core)
 
     for plane in range(planes):
         for x in range(2):
             s = 4 * plane + 2 * x + lax.rem(other, 2)
-            for part in (None, 0, 1):
+            for part in ((0, 0), (0, 1), (1, 0), (1, 1)):
                 arrive((), s, part)
 
     for d in OFFSETS:
@@ -276,8 +274,8 @@
         scratch_shapes=[
             pltpu.SemaphoreType.DMA((count, SLOTS)),
             pltpu.SemaphoreType.DMA((count, SLOTS)),
-            pltpu.SemaphoreType.DMA((n, 3, 5)),
-            pltpu.SemaphoreType.DMA((n, 3)),
+            pltpu.SemaphoreType.DMA((n, 4, 5)),
+            pltpu.SemaphoreType.DMA((n, 4)),
         ],
         compiler_params=pltpu.CompilerParams(
             collective_id=0, has_side_effects=True, vmem_limit_bytes=LIMIT

time: 170 us -> 166 us (0.976)
  Pallas kernels: 165 us -> 161 us
    pallas_call x1, Pallas kernels: 26.7 us -> 16.1 us  [halo(): pl.pallas_call(functools.partial(halo_kernel, count), out_shape=[jax.Shap...]
    pallas_call x1, Pallas kernels: 92.3 us -> 97.8 us  [gather_halo(): pl.pallas_call(functools.partial(gather_halo_kernel, count), out_shape=[j...]
where the time goes in v4:
time: 166 us; the launch traced here: 165 us
  Pallas kernels  161 us (97%)
  local copies, waits for them, and re-layouts  2.74 us (2%)
    pallas_call x1, Pallas kernels, gather_halo(): pl.pallas_call(functools.partial(gather_halo_kernel, count), out_shape=[j...  97.8 us
    pallas_call x3, Pallas kernels, call(): pl.pallas_call(kernel, out_shape=[jax.ShapeDtypeStruct(s, t) for s, t in...  36.9 us
    pallas_call x1, Pallas kernels, halo(): pl.pallas_call(functools.partial(halo_kernel, count), out_shape=[jax.Shap...  16.1 us
    pallas_call x1, Pallas kernels, total_rows(): pl.pallas_call(total_kernel, out_shape=jax.ShapeDtypeStruct(rows.shape, r...  10 us

profile of v4, /device:TPU:0, one launch (start us, length us, event | category | flops | bytes accessed | tf_op | source)
XLA Modules:
  0.0 165.5 jit_solution(6768066466957595025)
XLA Ops:
  0.6 0.0 copy-start.1
  0.6 0.0 copy-start.2
  0.7 1.1 slice_bitcast_fusion
  1.8 1.0 slice_bitcast_fusion.2
  2.8 0.1 pad_maximum_fusion
  3.5 0.0 copy-done.1
  3.5 97.8 %shard_map.94 = (bf16[16,80,2560]{2,1,0:T(8,128)(2,1)}, bf16[16,80,2560]{2,1,0:T(8,128)(2,1)}, bf16[9,128,1280]{2,1,0:T(8,128)(2,1)S(1)}, f32[9,8,128]{2,1,0:T(8,128)S(1)}) custom-call(bf16[80,2560]{1,0:T(8,128)(2,1)S(1)} %get-tuple-element.41.refs_0_, bf16[80,2560]{1,0:T(8,128)(2,1)S(1)} %get-tuple-element.42.refs_1_, bf16[128,1280]{1,0:T(8,128)(2,1)S(1)} %bitcast.21, ...), custom_call_target="tpu_custom_call" | custom-call | tf_op jit(solution)/shard_map/pallas_call | solution.py:268
  101.3 0.3 convert_reduce_fusion.tags
  101.6 0.0 copy-done.2
  101.6 0.0 copy-start.3
  101.6 0.0 copy-start
  101.6 11.3 %shard_map.95 = (bf16[640,1920]{1,0:T(8,128)(2,1)S(1)}, bf16[128,640]{1,0:T(8,128)(2,1)S(1)}, f32[128,8]{1,0:T(8,128)S(1)}, bf16[128,1280]{1,0:T(8,128)(2,1)S(1)}) custom-call(s32[9]{0:T(128)S(1)} %convert_reduce_fusion.tags, bf16[9,128,1280]{2,1,0:T(8,128)(2,1)S(1)} %get-tuple-element.21.near, bf16[1280,2560]{1,0:T(8,128)(2,1)} %bitcast.23, ...), custom_call_target="tpu_custom_call" | custom-call | flops 6442450944 | bytes 8388608 | tf_op jit(solution)/shard_map/pallas_call | solution.py:479
  112.9 0.0 copy-done.3
  112.9 0.1 fusion.1
  113.0 0.1 compare_convert_fusion.same
  113.1 0.0 copy-done
  113.1 15.6 %shard_map.96 = (bf16[128,1280]{1,0:T(8,128)(2,1)}, f32[128,1280]{1,0:T(8,128)S(1)}, bf16[128,640]{1,0:T(8,128)(2,1)S(1)}, f32[16,128]{1,0:T(8,128)S(1)}, f32[1,1280]{1,0:T(1,128)S(1)}) custom-call(bf16[128,1280]{1,0:T(8,128)(2,1)S(1)} %get-tuple-element.23.hidden_ref, bf16[128,1280]{1,0:T(8,128)(2,1)S(1)} %bitcast.20, ...), custom_call_target="tpu_custom_call" | custom-call | flops 3221225472 | bytes 8388608 | tf_op jit(solution)/shard_map/pallas_call | solution.py:479
  128.7 16.1 %shard_map.97 = (bf16[9,128,640]{2,1,0:T(8,128)(2,1)S(1)}, f32[9,16,128]{2,1,0:T(8,128)S(1)}) custom-call(bf16[128,640]{1,0:T(8,128)(2,1)S(1)} %get-tuple-element.29.refs_0_, f32[16,128]{1,0:T(8,128)S(1)} %get-tuple-element.30.refs_1_), custom_call_target="tpu_custom_call" | custom-call | tf_op jit(solution)/shard_map/pallas_call | solution.py:108
  144.8 10.0 %shard_map.98 = (f32[128,1280]{1,0:T(8,128)}, f32[1,1280]{1,0:T(1,128)S(1)}) custom-call(s32[9]{0:T(128)S(1)} %convert_reduce_fusion.tags, bf16[640,1920]{1,0:T(8,128)(2,1)S(1)} %get-tuple-element.28.packed, bf16[9,128,640]{2,1,0:T(8,128)(2,1)S(1)} %get-tuple-element.31.near_dout, f32[9,16,128]{2,1,0:T(8,128)S(1)} %get-tuple-element.32.near_stats, ...), custom_call_target="tpu_custom_call" | custom-call | flops 3221225472 | bytes 8388608 | tf_op jit(solution)/shard_map/pallas_call | solution.py:479
  154.8 10.0 %shard_map.99 = f32[2,1280]{1,0:T(2,128)S(1)} custom-call(f32[2,1280]{1,0:T(2,128)S(1)} %pad_maximum_fusion.2.row_ref), custom_call_target="tpu_custom_call" | custom-call | tf_op jit(solution)/shard_map/pallas_call | solution.py:329
  164.9 0.6 copy.12
  (3 shorter events, 0.0 us)
Async XLA Ops:
  0.6 2.9 %copy-start.1 = (bf16[1,128,1280]{2,1,0:T(8,128)(2,1)S(1)}, bf16[1,128,1280]{2,1,0:T(8,128)(2,1)}, u32[]{:S(2)}) copy-start(bf16[1,128,1280]{2,1,0:T(8,128)(2,1)} %param.7) | copy-start | bytes 983044
  0.6 100.9 %copy-start.2 = (f32[2,1280]{1,0:T(2,128)S(1)}, f32[2,1280]{1,0:T(2,128)}, u32[]{:S(2)}) copy-start(f32[2,1280]{1,0:T(2,128)} %gain.5) | copy-start | bytes 30724
  101.6 11.3 %copy-start.3 = (s32[1,1,128]{2,1,0:T(1,128)S(1)}, s32[1,1,128]{2,1,0:T(1,128)}, u32[]{:S(2)}) copy-start(s32[1,1,128]{2,1,0:T(1,128)} %param.10) | copy-start | bytes 1540
  101.6 11.5 %copy-start = (bf16[1,128,1280]{2,1,0:T(8,128)(2,1)S(1)}, bf16[1,128,1280]{2,1,0:T(8,128)(2,1)}, u32[]{:S(2)}) copy-start(bf16[1,128,1280]{2,1,0:T(8,128)(2,1)} %param.8) | copy-start | bytes 983044
